TPU v7x, 32 devices: a whole 2x2x4 slice. The times are simulated.
32 devices in a mesh: row: 8 (over z, core), col: 4 (over y, x), rep: 1.
Axes of the slice: x: 2, y: 2, z: 4, core: 2. Of those that a mesh axis runs over, the one named last changes fastest.
Arguments:
- momentum: float32 [1, 8192, 8192], P('rep', 'row', 'col'), may hold values from -6 to 6
- gradient: bfloat16 [1, 8192, 8192], P('rep', 'row', 'col'), may hold values from -6 to 6
- weight: float32 [8192, 8192], P('row', 'col'), may hold values from -0.0625 to 0.0625
- right_basis: float32 [8192, 256], P('col'), may hold values from -6 to 6
Outputs:
- new_momentum: float32 [1, 8192, 8192], P('rep', 'row', 'col')
- new_weight: float32 [8192, 8192], P('row', 'col')
- new_basis: float32 [8192, 256], P('col')
All inputs are finite; a program needn't handle non-finite values.
Results may differ from a plain program's by a relative error of at most 0.0012.
Values sent between devices are 32-bit elements; how exact they have to be, the bound alone decides.
No kernel may reach another device: no remote copies, remote signals or barrier semaphores. Data moves between devices by JAX's collectives and lax.ppermute only.
A program may use at most 128 MiB of HBM per device.

v0:
```python
import functools

import jax
import jax.numpy as jnp
from jax import lax
from jax.experimental import pallas as pl
from jax.experimental.pallas import tpu as pltpu
from jax.sharding import PartitionSpec as P

D = 8192
RANK = 256
ITERS = 2
HALF = RANK // 2
QUARTER = RANK // 4
PART = RANK // 8
SUB = 8
TILE = 256

beta_mom = 0.95
learn_rate = 0.05

F32 = jnp.float32
BF16 = jnp.bfloat16
HIGHEST = lax.Precision.HIGHEST
HIGH = lax.Precision.HIGH
NT = ((1,), (1,))
NN = ((1,), (0,))


def dot(a, b, dims=NN, precision=None):
    return lax.dot_general(a, b, (dims, ((), ())), precision=precision, preferred_element_type=F32)


def split(x):
    high = x.astype(BF16)
    return high, (x - high.astype(F32)).astype(BF16)


def dot3(a, b, dims=NN):
    return dot(a[0], b[0], dims) + (dot(a[1], b[0], dims) + dot(a[0], b[1], dims))


def call(kernel, name, flops, moved, **rest):
    rest.setdefault("compiler_params", pltpu.CompilerParams(vmem_limit_bytes=24 * 2**20))
    return pl.pallas_call(
        kernel,
        name=name,
        cost_estimate=pl.CostEstimate(flops=flops, bytes_accessed=moved, transcendentals=0),
        **rest,
    )


def shaped(*shape, dtype=F32):
    return jax.ShapeDtypeStruct(shape, dtype)


VMEM = pl.BlockSpec(memory_space=pltpu.VMEM)
SMEM = pl.BlockSpec(memory_space=pltpu.SMEM)


def inverse_factor(block):
    shape = (SUB, HALF)
    lanes = lax.broadcasted_iota(jnp.int32, shape, 1)
    subs = lax.broadcasted_iota(jnp.int32, shape, 0)
    count = HALF // SUB

    def spread(tile, lane):
        return jnp.broadcast_to(tile[:, lane:lane + 1], shape)

    def repeat(tile, sub):
        return jnp.broadcast_to(tile[sub:sub + 1, :], shape)

    tiles = [block[SUB * i:SUB * (i + 1), :] for i in range(count)]
    for t in range(count):
        low = SUB * t
        panel = jnp.logical_and(lanes >= low, lanes < low + SUB)
        cols = [spread(tiles[t], low + j) for j in range(SUB)]
        tile = jnp.where(panel, 0.0, tiles[t])
        scale, rows, upper = [], [], {}
        for j in range(SUB):
            r = lax.rsqrt(repeat(cols[j], j))
            mult = jnp.where(subs > j, cols[j] * r, 0.0)
            for k in range(j + 1, SUB):
                upper[j, k] = repeat(cols[k], j) * r
                cols[k] = cols[k] - mult * upper[j, k]
            row = jnp.where(lanes == low + j, r, repeat(tile, j) * r)
            tile = jnp.where(subs == j, row, tile - mult * row)
            scale.append(r)
            rows.append(row)
        tiles[t] = tile
        for i in range(t + 1, count):
            cols = [spread(tiles[i], low + j) for j in range(SUB)]
            tile = jnp.where(panel, 0.0, tiles[i])
            for j in range(SUB):
                mult = cols[j] * scale[j]
                for k in range(j + 1, SUB):
                    cols[k] = cols[k] - mult * upper[j, k]
                tile = tile - mult * rows[j]
            tiles[i] = tile
    full = jnp.concatenate(tiles, axis=0)
    down = lax.broadcasted_iota(jnp.int32, (HALF, HALF), 0)
    across = lax.broadcasted_iota(jnp.int32, (HALF, HALF), 1)
    return jnp.where(across <= down, full, 0.0)


def inverse_body(gram_ref, out_ref):
    first = inverse_factor(gram_ref[:HALF, :HALF])
    side = dot(gram_ref[HALF:, :HALF], first, NT, HIGHEST)
    rest = gram_ref[HALF:, HALF:] - dot(side, side, NT, HIGHEST)
    second = inverse_factor(rest)
    out_ref[:HALF, :HALF] = first
    out_ref[:HALF, HALF:] = jnp.zeros((HALF, HALF), F32)
    out_ref[HALF:, :HALF] = -dot(second, dot(side, first, precision=HIGHEST), precision=HIGHEST)
    out_ref[HALF:, HALF:] = second


def inverse_cholesky(gram):
    return call(
        inverse_body, "inverse_cholesky", 12_000_000_000, 2 * 4 * RANK * RANK,
        out_shape=shaped(RANK, RANK), in_specs=[VMEM], out_specs=VMEM,
    )(gram)


def place(out_ref, me, mine, other):
    for b in range(4):
        block = (mine, other)[b // 2][PART * (b % 2):PART * (b % 2 + 1), :]
        out_ref[pl.ds(pl.multiple_of((me ^ b) * PART, PART), PART), :] = block


def start_kernel(momentum_ref, gradient_ref, basis_ref, high_ref, low_ref, up0, down0, up1, down1, bhigh_ref, blow_ref):
    rows, cols = momentum_ref.shape
    count = up0.shape[0] // HALF

    def body(momentum, gradient, basis):
        step = pl.program_id(0)

        @pl.when(step == 0)
        def _():
            bhigh_ref[...], blow_ref[...] = split(basis[...])

        here = pl.ds(pl.multiple_of(step * HALF, HALF), HALF)
        buffer = split(momentum[...] + gradient[...].astype(F32))
        high_ref[here, :], low_ref[here, :] = buffer
        part = dot3(buffer, (bhigh_ref[...], blow_ref[...]))
        there = pl.ds(pl.multiple_of(lax.rem(step, count) * HALF, HALF), HALF)

        @pl.when(step < count)
        def _():
            up0[there, :] = part[:, :HALF]
            up1[there, :] = part[:, HALF:]

        @pl.when(step >= count)
        def _():
            down0[there, :] = part[:, :HALF]
            down1[there, :] = part[:, HALF:]

    block = pl.BlockSpec((HALF, cols), lambda i: (i, 0))
    pltpu.emit_pipeline(
        body, grid=(rows // HALF,), in_specs=[block, block, pl.BlockSpec((cols, RANK), lambda i: (0, 0))],
    )(momentum_ref, gradient_ref, basis_ref)


def start(*args):
    rows, cols = args[0].shape
    return call(
        start_kernel, "start", 6 * rows * cols * RANK, 6 * rows * cols,
        out_shape=[shaped(rows, cols, dtype=BF16)] * 2 + [shaped(rows // 2, HALF)] * 4,
        in_specs=[pl.BlockSpec(memory_space=pltpu.HBM)] * 3, out_specs=[VMEM] * 6,
        scratch_shapes=[pltpu.VMEM((cols, RANK), BF16)] * 2,
    )(*(pltpu.with_memory_space_constraint(x, pltpu.HBM) for x in args))


def left_kernel(high_ref, low_ref, factor_ref, *refs):
    up_ref, down_ref = refs[-2:]
    half = down_ref.shape[0]

    for ref, base in ((up_ref, 0), (down_ref, half)):
        @pl.loop(0, half // TILE)
        def _(c):
            here = pl.ds(pl.multiple_of(base + c * TILE, TILE), TILE)
            both = dot(high_ref[here, :], factor_ref[...], NT)
            part = (both[:, :HALF] + both[:, HALF:]) + dot(low_ref[here, :], factor_ref[:HALF, :], NT)
            ref[pl.ds(pl.multiple_of(c * TILE, TILE), TILE), :] = part

    if len(refs) == 3:
        up_ref[half:, :] = refs[0][...]


def left_product(buffer, factor, square):
    rows, cols = buffer[0].shape
    return call(
        left_kernel, "left", 4 * rows * cols * RANK, 4 * rows * cols,
        out_shape=[shaped(rows // 2 + SUB, HALF), shaped(rows // 2, HALF)], in_specs=[VMEM] * 4, out_specs=[VMEM] * 2,
    )(*buffer, factor, square)


def product_kernel(first, scaled, me_ref, *refs):
    before, refs = ((), refs) if first else (refs[:1], refs[1:])
    up, up_more, down, down_more, high_ref, low_ref, keep_ref, give_ref, left_ref, plain_ref, turned_ref, pair_ref = refs
    rows = down.shape[0]
    top, bottom = up[:rows, :] + up_more[:rows, :], down[...] + down_more[...]
    if scaled:
        total = up[rows:rows + 1, :] + up_more[rows:rows + 1, :]
        scale = 1.0 / jnp.sqrt(total / F32(D) + F32(1e-06))
        top, bottom = top * scale, bottom * scale
    left_ref[:rows, :] = top
    left_ref[rows:, :] = bottom
    plain_ref[:, :rows] = top.T
    plain_ref[:, rows:] = bottom.T
    me = me_ref[0]
    for b in range(4):
        block = plain_ref[pl.ds(pl.multiple_of((me ^ b) * PART, PART), PART), :]
        turned_ref[PART * b:PART * (b + 1), :] = block
        pair_ref[PART * b:PART * (b + 1), :], pair_ref[HALF + PART * b:HALF + PART * (b + 1), :] = split(block)
    spot = 0
    for ref in (*before, left_ref):
        gram = dot(turned_ref[...], ref[...], precision=HIGHEST)
        keep_ref[:, spot:spot + HALF] = gram[:QUARTER]
        give_ref[:, spot:spot + HALF] = gram[QUARTER:]
        spot += HALF
    step = 2 * TILE

    @pl.loop(0, high_ref.shape[1] // step)
    def _(c):
        lanes = pl.ds(pl.multiple_of(c * step, step), step)
        both = dot(pair_ref[...], high_ref[:, lanes])
        part = (both[:HALF] + both[HALF:]) + dot(pair_ref[:HALF, :], low_ref[:, lanes])
        lanes = pl.ds(pl.multiple_of(spot + c * step, HALF), step)
        keep_ref[:, lanes] = part[:QUARTER]
        give_ref[:, lanes] = part[QUARTER:]


def product(scaled, me, before, parts, buffer):
    rows, cols = buffer[0].shape
    width = HALF * (len(before) + 1) + cols
    return call(
        functools.partial(product_kernel, not before, scaled), "product", 4 * rows * width * RANK, 4 * rows * width,
        out_shape=[shaped(QUARTER, width)] * 2 + [shaped(rows, HALF)],
        in_specs=[SMEM] + [VMEM] * (6 + len(before)), out_specs=[VMEM] * 3,
        scratch_shapes=[pltpu.VMEM((HALF, rows), F32)] * 2 + [pltpu.VMEM((RANK, rows), BF16)],
    )(me, *before, *parts, *buffer)


def solved(inverse, wide_ref, out_ref, pair_ref):
    inverse = split(inverse)
    square = jnp.zeros((HALF, 1), F32)
    step = 2 * TILE
    for c in range(wide_ref.shape[1] // step):
        lanes = pl.ds(step * c, step)
        part = dot3(inverse, split(wide_ref[:, lanes]))
        out_ref[:, lanes] = part
        pair_ref[:HALF, lanes], pair_ref[HALF:, lanes] = split(part)
        square = square + jnp.sum(part * part, axis=1, keepdims=True)
    return jnp.broadcast_to(square, (HALF, HALF)).T[:SUB, :]


def first_kernel(me_ref, mine_ref, other_ref, inverse_ref, wide_ref, out_ref, pair_ref, square_ref, gram_ref):
    me = me_ref[0]
    place(gram_ref, me, mine_ref[:, :HALF], other_ref[:, :HALF])
    place(wide_ref, me, mine_ref[:, HALF:], other_ref[:, HALF:])
    inverse_ref[...] = inverse_factor(gram_ref[...])
    square_ref[...] = solved(inverse_ref[...], wide_ref, out_ref, pair_ref)


def first_solve(me, mine, other):
    cols = mine.shape[1] - HALF
    return call(
        first_kernel, "first_solve", 5_000_000_000, 20 * HALF * cols,
        out_shape=[shaped(HALF, HALF), shaped(HALF, cols), shaped(HALF, cols), shaped(RANK, cols, dtype=BF16), shaped(SUB, HALF)],
        in_specs=[SMEM, VMEM, VMEM], out_specs=[VMEM] * 5, scratch_shapes=[pltpu.VMEM((HALF, HALF), F32)],
    )(me, mine, other)


def second_kernel(me_ref, mine_ref, other_ref, first_ref, wide0_ref, inverse_ref, out_ref, pair_ref, square_ref, gram_ref, wide_ref):
    me = me_ref[0]
    place(gram_ref, me, mine_ref[:, :RANK], other_ref[:, :RANK])
    place(wide_ref.at[HALF:, :], me, mine_ref[:, RANK:], other_ref[:, RANK:])
    wide_ref[:HALF, :] = wide0_ref[...]
    first = first_ref[...]
    side = dot(gram_ref[:, :HALF], first, NT, HIGHEST)
    second = inverse_factor(gram_ref[:, HALF:] - dot(side, side, NT, HIGHEST))
    inverse_ref[:HALF, :HALF] = first
    inverse_ref[:HALF, HALF:] = jnp.zeros((HALF, HALF), F32)
    inverse_ref[HALF:, :HALF] = -dot(second, dot(side, first, precision=HIGHEST), precision=HIGHEST)
    inverse_ref[HALF:, HALF:] = second
    square_ref[...] = solved(inverse_ref[HALF:, :], wide_ref, out_ref, pair_ref)


def second_solve(me, mine, other, first, wide0):
    cols = mine.shape[1] - RANK
    return call(
        second_kernel, "second_solve", 6_000_000_000, 20 * HALF * cols,
        out_shape=[shaped(RANK, RANK), shaped(HALF, cols), shaped(RANK, cols, dtype=BF16), shaped(SUB, HALF)],
        in_specs=[SMEM] + [VMEM] * 4, out_specs=[VMEM] * 4,
        scratch_shapes=[pltpu.VMEM((HALF, RANK), F32), pltpu.VMEM((RANK, cols), F32)],
    )(me, mine, other, first, wide0)


def momentum_kernel(left0_ref, left1_ref, inverse_ref, pair0_ref, pair1_ref, high_ref, low_ref, out_ref, ortho_ref, half_ref):
    step, width = pl.program_id(0), out_ref.shape[1]

    @pl.when(step == 0)
    def _():
        left = jnp.concatenate([left0_ref[...], left1_ref[...]], axis=1)
        ortho = dot3(split(left), split(inverse_ref[...]), NT)
        ortho_ref[...] = ortho
        half_ref[...] = ortho.astype(BF16)

    lanes = pl.ds(pl.multiple_of(step * width, width), width)
    factor = jnp.concatenate([pair0_ref[:HALF, lanes], pair1_ref[:HALF, lanes]], axis=0)
    feedback = F32(1.0 - beta_mom) * dot(half_ref[...], factor)
    out_ref[...] = (high_ref[:, lanes].astype(F32) + low_ref[:, lanes].astype(F32)) - feedback


def momentum_update(lefts, inverse, pairs, buffer):
    rows, cols = buffer[0].shape
    return call(
        momentum_kernel, "momentum", 2 * rows * cols * RANK, 4 * rows * cols,
        out_shape=[shaped(rows, cols), shaped(rows, RANK)], grid=(cols // TILE,),
        in_specs=[VMEM] * 7, out_specs=[pl.BlockSpec((rows, TILE), lambda i: (0, i)), VMEM],
        scratch_shapes=[pltpu.VMEM((rows, RANK), BF16)],
    )(*lefts, inverse, *pairs, *buffer)


def weight_kernel(ortho_ref, s0, s1, s2, s3, pair0_ref, pair1_ref, factor0_ref, factor1_ref, weight_ref, out_ref, basis_ref, high_ref, low_ref):
    total = (s0[0:1, :] + s1[0:1, :]) + (s2[0:1, :] + s3[0:1, :])
    scale = 1.0 / jnp.sqrt(total / F32(D) + F32(1e-06))
    step, width = pl.program_id(0), out_ref.shape[1]

    @pl.when(step == 0)
    def _():
        high_ref[...], low_ref[...] = split(ortho_ref[...] * (scale * F32(learn_rate * (D / RANK) ** 0.5)))

    lanes = pl.ds(pl.multiple_of(step * width, width), width)
    fhigh = jnp.concatenate([pair0_ref[:HALF, lanes], pair1_ref[:HALF, lanes]], axis=0)
    flow = jnp.concatenate([pair0_ref[HALF:, lanes], pair1_ref[HALF:, lanes]], axis=0)
    out_ref[...] = weight_ref[:, lanes] - dot3((high_ref[...], low_ref[...]), (fhigh, flow))
    basis_ref[:, :HALF] = factor0_ref[:, lanes].T * scale[:, :HALF]
    basis_ref[:, HALF:] = factor1_ref[:, lanes].T * scale[:, HALF:]


def weight_update(ortho, squares, pairs, factors, weight):
    rows, cols = weight.shape
    return call(
        weight_kernel, "weight", 6 * rows * cols * RANK, 4 * rows * cols,
        out_shape=[shaped(rows, cols), shaped(cols, RANK)], grid=(cols // TILE,), in_specs=[VMEM] * 10,
        out_specs=[pl.BlockSpec((rows, TILE), lambda i: (0, i)), pl.BlockSpec((TILE, RANK), lambda i: (i, 0))],
        scratch_shapes=[pltpu.VMEM((rows, RANK), BF16)] * 2,
    )(ortho, *squares, *pairs, *factors, weight)


def swap(x, axis, bit):
    size = lax.axis_size(axis)
    return lax.ppermute(x, axis, [(i, i ^ bit) for i in range(size)])


def together(*arrays):
    return lax.optimization_barrier(arrays)


def tuned(momentum, gradient, weight, right_basis):
    row = lax.axis_index("row")
    me = (2 * (row & 1) + ((row >> 1) & 1)).astype(jnp.int32)[None]
    high, low, up0, down0, up1, down1 = start(momentum[0], gradient[0], right_basis)
    buffer = (high, low)
    got0 = swap(up0, "col", 1), swap(down0, "col", 2)
    up0, down0, got0, up1, down1 = together(up0, down0, got0, up1, down1)
    for sweep in range(ITERS):
        last, scaled = sweep == ITERS - 1, sweep > 0

        up0, down0 = up0 + got0[0], down0 + got0[1]
        got0 = swap(up0, "col", 2), swap(down0, "col", 1)
        if sweep:
            up1, down1 = left_product(buffer, split1, square1)
        got1 = swap(up1, "col", 1), swap(down1, "col", 2)
        up0, down0, got0, up1, down1, got1 = together(up0, down0, got0, up1, down1, got1)

        up1, down1 = up1 + got1[0], down1 + got1[1]
        got1 = swap(up1, "col", 2), swap(down1, "col", 1)
        keep0, give0, left0 = product(scaled, me, (), (up0, got0[0], down0, got0[1]), buffer)
        core0 = swap(give0, "row", 1)
        up1, down1, got1, keep0, core0, left0 = together(up1, down1, got1, keep0, core0, left0)

        part0 = keep0 + core0
        pair0 = swap(part0[PART:], "row", 2)
        keep1, give1, left1 = product(scaled, me, (left0,), (up1, got1[0], down1, got1[1]), buffer)
        core1 = swap(give1, "row", 1)
        part0, pair0, keep1, core1 = together(part0, pair0, keep1, core1)

        side0 = part0[:PART] + pair0
        cross0 = swap(side0, "row", 4)
        part1 = keep1 + core1
        pair1 = swap(part1[PART:], "row", 2)
        side0, cross0, part1, pair1 = together(side0, cross0, part1, pair1)

        total0 = side0 + cross0
        back0 = swap(total0, "row", 2)
        side1 = part1[:PART] + pair1
        cross1 = swap(side1, "row", 4)
        total0, back0, side1, cross1 = together(total0, back0, side1, cross1)

        mine0 = jnp.concatenate([total0, back0], axis=0)
        other0 = swap(mine0, "row", 1)
        total1 = side1 + cross1
        back1 = swap(total1, "row", 2)
        first, wide, factor0, split0, square0 = first_solve(me, mine0, other0)
        total1, back1, first, wide, split0, square0 = together(total1, back1, first, wide, split0, square0)

        mine1 = jnp.concatenate([total1, back1], axis=0)
        other1 = swap(mine1, "row", 1)
        if not last:
            up0, down0 = left_product(buffer, split0, square0)
            got0 = swap(up0, "col", 1), swap(down0, "col", 2)
        inverse, factor1, split1, square1 = second_solve(me, mine1, other1, first, wide)
        if not last:
            up0, down0, got0, split1, square1 = together(up0, down0, got0, split1, square1)

    square = jnp.concatenate([square0, square1], axis=1)
    squares = (square, swap(square, "col", 1), swap(square, "col", 2), swap(square, "col", 3))
    new_momentum, ortho = momentum_update((left0, left1), inverse, (split0, split1), buffer)
    new_weight, new_basis = weight_update(ortho, squares, (split0, split1), (factor0, factor1), weight)
    return new_momentum[None], new_weight, new_basis


def general(momentum, gradient, weight, right_basis):
    replicas = lax.axis_size("rep")
    buffer = momentum[0] + gradient[0].astype(F32)
    basis, dims = right_basis, NN
    for sweep in range(ITERS):
        left = lax.psum(dot(buffer, basis, dims, HIGH) / replicas, ("col", "rep"))
        if sweep:
            left = left / rms
        gram = lax.psum(dot(left, left, ((0,), (0,)), HIGHEST), "row")
        wide = lax.psum(dot(left, buffer, ((0,), (0,)), HIGH) / replicas, ("row", "rep"))
        inverse = inverse_cholesky(gram)
        factor = dot(inverse, wide, precision=HIGHEST)
        rms = jnp.sqrt(lax.psum(jnp.sum(factor * factor, axis=1)[None, :], "col") / F32(D) + 1e-06)
        basis, dims = factor, NT
    ortho = dot(left, inverse, NT, HIGHEST)
    new_momentum = (buffer - (1.0 - beta_mom) * dot(ortho, factor, precision=HIGH))[None]
    basis = factor / rms.T
    new_weight = weight - learn_rate * jnp.sqrt(F32(D) / F32(RANK)) * dot(ortho, basis, precision=HIGH)
    return new_momentum, new_weight, basis.T


def solution(mesh):
    sizes = dict(mesh.shape)
    fits = sizes["row"] == 8 and sizes["col"] == 4 and sizes["rep"] == 1
    return jax.shard_map(
        tuned if fits else general,
        mesh=mesh,
        in_specs=(P("rep", "row", "col"), P("rep", "row", "col"), P("row", "col"), P("col", None)),
        out_specs=(P("rep", "row", "col"), P("row", "col"), P("col", None)),
        check_vma=False,
    )
```

profile of v0, /device:TPU:0, one launch (start us, length us, event | category | flops | bytes accessed | tf_op | source)
XLA Modules:
  0.0 230.2 jit_solution(15665111937233607047)
XLA Ops:
  0.6 10.8 %start.1 = (bf16[1024,2048]{1,0:T(8,128)(2,1)S(1)}, bf16[1024,2048]{1,0:T(8,128)(2,1)S(1)}, f32[512,128]{1,0:T(8,128)S(1)}, f32[512,128]{1,0:T(8,128)S(1)}, f32[...) custom-call(f32[1024,2048]{1,0:T(8,128)} %bitcast.6, bf16[1024,2048]{1,0:T(8,128)(2,1)} %bitcast.7, f32[2048,256]{1,0:T(8,128)} %basis_ref.1), custom_call_target="tpu_custom_call" | custom-call | flops 3221225472 | bytes 12582912 | tf_op jit(solution)/shard_map/start/pallas_call | solution.py:165
  20.0 4.8 %collective-permute-done = f32[512,128]{1,0:T(8,128)S(1)} collective-permute-done((f32[512,128]{1,0:T(8,128)S(1)}, f32[512,128]{1,0:T(8,128)S(1)}, u32[]{:S(2)}, u32[]{:S(2)}) %collective-permute-start) | collective-permute-done | bytes 262176 | tf_op jit(solution)/shard_map/ppermute | solution.py:354
  30.5 5.1 %collective-permute-done.3.refs_3_ = f32[512,128]{1,0:T(8,128)S(1)} collective-permute-done((f32[512,128]{1,0:T(8,128)S(1)}, f32[512,128]{1,0:T(8,128)S(1)}, u32[]{:S(2)}, u32[]{:S(2)}) %collective-permute-start.3) | collective-permute-done | bytes 262176 | tf_op jit(solution)/shard_map/ppermute | solution.py:354
  43.6 3.1 %product.4 = (f32[64,2176]{1,0:T(8,128)S(1)}, f32[64,2176]{1,0:T(8,128)S(1)}, f32[1024,128]{1,0:T(8,128)S(1)}) custom-call(s32[1]{0:T(128)} %bitcast.2.me_ref, f32[512,128]{1,0:T(8,128)S(1)} %add.63.refs_0_, f32[512,128]{1,0:T(8,128)S(1)} %collective-permute-done.2.refs_1_, f32[512,128]{1,0:T(8,128)S(1)} %add.64.refs_2_, ...), custom_call_target="tpu_custom_call" | custom-call | flops 2281701376 | bytes 8912896 | tf_op jit(solution)/shard_map/product/pallas_call | solution.py:236
  49.9 5.7 %collective-permute-done.7.refs_4_ = f32[512,128]{1,0:T(8,128)S(1)} collective-permute-done((f32[512,128]{1,0:T(8,128)S(1)}, f32[512,128]{1,0:T(8,128)S(1)}, u32[]{:S(2)}, u32[]{:S(2)}) %collective-permute-start.7) | collective-permute-done | bytes 262176 | tf_op jit(solution)/shard_map/ppermute | solution.py:354
  56.8 3.8 %product.5 = (f32[64,2304]{1,0:T(8,128)S(1)}, f32[64,2304]{1,0:T(8,128)S(1)}, f32[1024,128]{1,0:T(8,128)}) custom-call(s32[1]{0:T(128)} %bitcast.2.me_ref, f32[1024,128]{1,0:T(8,128)S(1)} %get-tuple-element.146.refs_0_, f32[512,128]{1,0:T(8,128)S(1)} %add.65.refs_1_, f32[512,128]{1,0:T(8,128)S(1)} %collective-permute-done.6.refs_2_, ...), custom_call_target="tpu_custom_call" | custom-call | flops 2415919104 | bytes 9437184 | tf_op jit(solution)/shard_map/product/pallas_call | solution.py:236
  62.3 7.5 %collective-permute-done.9 = f32[32,2176]{1,0:T(8,128)S(1)} collective-permute-done((f32[32,2176]{1,0:T(8,128)S(1)}, f32[32,2176]{1,0:T(8,128)S(1)}, u32[]{:S(2)}, u32[]{:S(2)}) %collective-permute-start.9) | collective-permute-done | bytes 278560 | tf_op jit(solution)/shard_map/ppermute | solution.py:354
  74.3 9.5 %collective-permute-done.11 = f32[32,2176]{1,0:T(8,128)S(1)} collective-permute-done((f32[32,2176]{1,0:T(8,128)S(1)}, f32[32,2176]{1,0:T(8,128)S(1)}, u32[]{:S(2)}, u32[]{:S(2)}) %collective-permute-start.11) | collective-permute-done | bytes 278560 | tf_op jit(solution)/shard_map/ppermute | solution.py:354
  89.9 8.7 %collective-permute-done.13 = f32[32,2176]{1,0:T(8,128)S(1)} collective-permute-done((f32[32,2176]{1,0:T(8,128)S(1)}, f32[32,2176]{1,0:T(8,128)S(1)}, u32[]{:S(2)}, u32[]{:S(2)}) %collective-permute-start.13) | collective-permute-done | bytes 278560 | tf_op jit(solution)/shard_map/ppermute | solution.py:354
  101.8 5.6 %first_solve.2 = (f32[128,128]{1,0:T(8,128)S(1)}, f32[128,2048]{1,0:T(8,128)S(1)}, f32[128,2048]{1,0:T(8,128)}, bf16[256,2048]{1,0:T(8,128)(2,1)S(1)}, f32[8,128]{1,0:T(8,128)S(1)}) custom-call(s32[1]{0:T(128)} %bitcast.2.me_ref, f32[64,2176]{1,0:T(8,128)S(1)} %constant_dynamic-update-slice_fusion.mine_ref, f32[64,2176]{1,0:T(8,128)S(1)} %collective-permute-done.16.other_ref), custom_call_target="tpu_custom_call" | custom-call | flops 5000000000 | bytes 5242880 | tf_op jit(solution)/shard_map/first_solve/pallas_call | solution.py:267
  109.5 3.1 %left.2 = (f32[520,128]{1,0:T(8,128)S(1)}, f32[512,128]{1,0:T(8,128)S(1)}) custom-call(bf16[1024,2048]{1,0:T(8,128)(2,1)S(1)} %copy-done.2, bf16[1024,2048]{1,0:T(8,128)(2,1)S(1)} %copy-done.5, bf16[256,2048]{1,0:T(8,128)(2,1)S(1)} %get-tuple-element.169.factor_ref, f32[8,128]{1,0:T(8,128)S(1)} %get-tuple-element.170.refs_0_), custom_call_target="tpu_custom_call" | custom-call | flops 2147483648 | bytes 8388608 | tf_op jit(solution)/shard_map/left/pallas_call | solution.py:191
  114.9 6.6 %second_solve.2 = (f32[256,256]{1,0:T(8,128)}, f32[128,2048]{1,0:T(8,128)}, bf16[256,2048]{1,0:T(8,128)(2,1)S(1)}, f32[8,128]{1,0:T(8,128)S(1)}) custom-call(s32[1]{0:T(128)} %bitcast.2.me_ref, f32[64,2304]{1,0:T(8,128)S(1)} %constant_dynamic-update-slice_fusion.2.mine_ref, f32[64,2304]{1,0:T(8,128)S(1)} %collective-permute-done.19.other_ref, ...), custom_call_target="tpu_custom_call" | custom-call | flops 6000000000 | bytes 5242880 | tf_op jit(solution)/shard_map/second_solve/pallas_call | solution.py:291
  123.4 2.9 %left.3 = (f32[520,128]{1,0:T(8,128)S(1)}, f32[512,128]{1,0:T(8,128)S(1)}) custom-call(bf16[1024,2048]{1,0:T(8,128)(2,1)S(1)} %copy-done.2, bf16[1024,2048]{1,0:T(8,128)(2,1)S(1)} %copy-done.5, bf16[256,2048]{1,0:T(8,128)(2,1)S(1)} %get-tuple-element.183.factor_ref, f32[8,128]{1,0:T(8,128)S(1)} %get-tuple-element.184.refs_0_), custom_call_target="tpu_custom_call" | custom-call | flops 2147483648 | bytes 8388608 | tf_op jit(solution)/shard_map/left/pallas_call | solution.py:191
  130.0 9.4 %collective-permute-done.21.refs_3_ = f32[512,128]{1,0:T(8,128)S(1)} collective-permute-done((f32[512,128]{1,0:T(8,128)S(1)}, f32[512,128]{1,0:T(8,128)S(1)}, u32[]{:S(2)}, u32[]{:S(2)}) %collective-permute-start.21) | collective-permute-done | bytes 262176 | tf_op jit(solution)/shard_map/ppermute | solution.py:354
  139.4 3.1 %product.6 = (f32[64,2176]{1,0:T(8,128)S(1)}, f32[64,2176]{1,0:T(8,128)S(1)}, f32[1024,128]{1,0:T(8,128)S(1)}) custom-call(s32[1]{0:T(128)} %bitcast.2.me_ref, f32[520,128]{1,0:T(8,128)S(1)} %add.74.refs_0_, f32[520,128]{1,0:T(8,128)S(1)} %collective-permute-done.20.refs_1_, f32[512,128]{1,0:T(8,128)S(1)} %add.75.refs_2_, ...), custom_call_target="tpu_custom_call" | custom-call | flops 2281701376 | bytes 8912896 | tf_op jit(solution)/shard_map/product/pallas_call | solution.py:236
  145.0 7.7 %collective-permute-done.25.refs_4_ = f32[512,128]{1,0:T(8,128)S(1)} collective-permute-done((f32[512,128]{1,0:T(8,128)S(1)}, f32[512,128]{1,0:T(8,128)S(1)}, u32[]{:S(2)}, u32[]{:S(2)}) %collective-permute-start.25) | collective-permute-done | bytes 262176 | tf_op jit(solution)/shard_map/ppermute | solution.py:354
  152.8 3.8 %product.7 = (f32[64,2304]{1,0:T(8,128)S(1)}, f32[64,2304]{1,0:T(8,128)S(1)}, f32[1024,128]{1,0:T(8,128)S(1)}) custom-call(s32[1]{0:T(128)} %bitcast.2.me_ref, f32[1024,128]{1,0:T(8,128)S(1)} %get-tuple-element.198.refs_0_.left0_ref, f32[520,128]{1,0:T(8,128)S(1)} %add.76.refs_1_, f32[520,128]{1,0:T(8,128)S(1)} %collective-permute-done.24.refs_2_, ...), custom_call_target="tpu_custom_call" | custom-call | flops 2415919104 | bytes 9437184 | tf_op jit(solution)/shard_map/product/pallas_call | solution.py:236
  158.1 7.8 %collective-permute-done.27 = f32[32,2176]{1,0:T(8,128)S(1)} collective-permute-done((f32[32,2176]{1,0:T(8,128)S(1)}, f32[32,2176]{1,0:T(8,128)S(1)}, u32[]{:S(2)}, u32[]{:S(2)}) %collective-permute-start.27) | collective-permute-done | bytes 278560 | tf_op jit(solution)/shard_map/ppermute | solution.py:354
  169.3 10.2 %collective-permute-done.29 = f32[32,2176]{1,0:T(8,128)S(1)} collective-permute-done((f32[32,2176]{1,0:T(8,128)S(1)}, f32[32,2176]{1,0:T(8,128)S(1)}, u32[]{:S(2)}, u32[]{:S(2)}) %collective-permute-start.29) | collective-permute-done | bytes 278560 | tf_op jit(solution)/shard_map/ppermute | solution.py:354
  185.6 8.7 %collective-permute-done.31 = f32[32,2176]{1,0:T(8,128)S(1)} collective-permute-done((f32[32,2176]{1,0:T(8,128)S(1)}, f32[32,2176]{1,0:T(8,128)S(1)}, u32[]{:S(2)}, u32[]{:S(2)}) %collective-permute-start.31) | collective-permute-done | bytes 278560 | tf_op jit(solution)/shard_map/ppermute | solution.py:354
  197.8 4.8 %first_solve.3 = (f32[128,128]{1,0:T(8,128)S(1)}, f32[128,2048]{1,0:T(8,128)S(1)}, f32[128,2048]{1,0:T(8,128)S(1)}, bf16[256,2048]{1,0:T(8,128)(2,1)S(1)}, f32[8,128]{1,0:T(8,128)S(1)}) custom-call(s32[1]{0:T(128)} %bitcast.2.me_ref, f32[64,2176]{1,0:T(8,128)S(1)} %constant_dynamic-update-slice_fusion.4.mine_ref, ...), custom_call_target="tpu_custom_call" | custom-call | flops 5000000000 | bytes 5242880 | tf_op jit(solution)/shard_map/first_solve/pallas_call | solution.py:267
  207.5 5.7 %second_solve.3 = (f32[256,256]{1,0:T(8,128)S(1)}, f32[128,2048]{1,0:T(8,128)S(1)}, bf16[256,2048]{1,0:T(8,128)(2,1)S(1)}, f32[8,128]{1,0:T(8,128)S(1)}) custom-call(s32[1]{0:T(128)} %bitcast.2.me_ref, f32[64,2304]{1,0:T(8,128)S(1)} %constant_dynamic-update-slice_fusion.6.mine_ref, f32[64,2304]{1,0:T(8,128)S(1)} %collective-permute-done.35.other_ref, ...), custom_call_target="tpu_custom_call" | custom-call | flops 6000000000 | bytes 5242880 | tf_op jit(solution)/shard_map/second_solve/pallas_call | solution.py:291
  216.7 6.1 %momentum.1 = (f32[1024,2048]{1,0:T(8,128)}, f32[1024,256]{1,0:T(8,128)S(1)}) custom-call(f32[1024,128]{1,0:T(8,128)S(1)} %get-tuple-element.198.refs_0_.left0_ref, f32[1024,128]{1,0:T(8,128)S(1)} %get-tuple-element.203.left1_ref, f32[256,256]{1,0:T(8,128)S(1)} %get-tuple-element.228.inverse_ref, bf16[256,2048]{1,0:T(8,128)(2,1)S(1)} %get-tuple-element.229.pair0_ref, ...), custom_call_target="tpu_custom_call" | custom-call | flops 1073741824 | bytes 8388608 | tf_op jit(solution)/shard_map/momentum/pallas_call | solution.py:317
  222.8 7.4 %weight.1 = (f32[1024,2048]{1,0:T(8,128)}, f32[2048,256]{1,0:T(8,128)}) custom-call(f32[1024,256]{1,0:T(8,128)S(1)} %get-tuple-element.232.ortho_ref, f32[8,256]{1,0:T(8,128)S(1)} %constant_dynamic-update-slice_fusion.8.s0, f32[8,256]{1,0:T(8,128)S(1)} %collective-permute-done.36.s1, f32[8,256]{1,0:T(8,128)S(1)} %collective-permute-done.37.s2, ...), custom_call_target="tpu_custom_call" | custom-call | flops 3221225472 | bytes 8388608 | tf_op jit(solution)/shard_map/weight/pallas_call | solution.py:344
  (118 shorter events, 77.4 us)
Async XLA Ops:
  15.5 9.2 %collective-permute-start = (f32[512,128]{1,0:T(8,128)S(1)}, f32[512,128]{1,0:T(8,128)S(1)}, u32[]{:S(2)}, u32[]{:S(2)}) collective-permute-start(f32[512,128]{1,0:T(8,128)S(1)} %get-tuple-element.127), channel_id=1, source_target_pairs={{0,1},{1,0},{2,3},{3,2},{4,5},{5,4},{6,7},{7,6},{8,9},{9,8},{10,11... | collective-permute-start | bytes 786440 | tf_op jit(solution)/shard_map/ppermute | solution.py:354
  26.3 9.3 %collective-permute-start.3 = (f32[512,128]{1,0:T(8,128)S(1)}, f32[512,128]{1,0:T(8,128)S(1)}, u32[]{:S(2)}, u32[]{:S(2)}) collective-permute-start(f32[512,128]{1,0:T(8,128)S(1)} %add.64.refs_2_), channel_id=1, source_target_pairs={{0,1},{1,0},{2,3},{3,2},{4,5},{5,4},{6,7},{7,6},{8,9},{9,8},{10,11... | collective-permute-start | bytes 786440 | tf_op jit(solution)/shard_map/ppermute | solution.py:354
  26.7 9.3 %collective-permute-start.2 = (f32[512,128]{1,0:T(8,128)S(1)}, f32[512,128]{1,0:T(8,128)S(1)}, u32[]{:S(2)}, u32[]{:S(2)}) collective-permute-start(f32[512,128]{1,0:T(8,128)S(1)} %add.63.refs_0_), channel_id=1, source_target_pairs={{0,2},{1,3},{2,0},{3,1},{4,6},{5,7},{6,4},{7,5},{8,10},{9,11},{10,... | collective-permute-start | bytes 786440 | tf_op jit(solution)/shard_map/ppermute | solution.py:354
  28.5 10.3 %collective-permute-start.4 = (f32[512,128]{1,0:T(8,128)S(1)}, f32[512,128]{1,0:T(8,128)S(1)}, u32[]{:S(2)}, u32[]{:S(2)}) collective-permute-start(f32[512,128]{1,0:T(8,128)S(1)} %get-tuple-element.133), channel_id=1, source_target_pairs={{0,1},{1,0},{2,3},{3,2},{4,5},{5,4},{6,7},{7,6},{8,9},{9,8},{10,11... | collective-permute-start | bytes 786440 | tf_op jit(solution)/shard_map/ppermute | solution.py:354
  30.0 9.3 %collective-permute-start.5 = (f32[512,128]{1,0:T(8,128)S(1)}, f32[512,128]{1,0:T(8,128)S(1)}, u32[]{:S(2)}, u32[]{:S(2)}) collective-permute-start(f32[512,128]{1,0:T(8,128)S(1)} %get-tuple-element.135), channel_id=1, source_target_pairs={{0,2},{1,3},{2,0},{3,1},{4,6},{5,7},{6,4},{7,5},{8,10},{9,11},{10,... | collective-permute-start | bytes 786440 | tf_op jit(solution)/shard_map/ppermute | solution.py:354
  46.7 10.1 %collective-permute-start.8 = (f32[64,2176]{1,0:T(8,128)S(1)}, f32[64,2176]{1,0:T(8,128)S(1)}, u32[]{:S(2)}, u32[]{:S(2)}) collective-permute-start(f32[64,2176]{1,0:T(8,128)S(1)} %get-tuple-element.142), channel_id=1, source_target_pairs={{0,4},{4,0},{8,12},{12,8},{16,20},{20,16},{24,28},{28,24},{1,5},{5... | collective-permute-start | bytes 1671176 | tf_op jit(solution)/shard_map/ppermute | solution.py:354
  69.9 14.7 %collective-permute-start.12 = (f32[32,2304]{1,0:T(8,128)S(1)}, f32[32,2304]{1,0:T(8,128)S(1)}, u32[]{:S(2)}, u32[]{:S(2)}) collective-permute-start(f32[32,2304]{1,0:T(8,128)S(1)} %slice.33), channel_id=1, source_target_pairs={{0,8},{4,12},{8,0},{12,4},{16,24},{20,28},{24,16},{28,20},{1,9},{5... | collective-permute-start | bytes 884744 | tf_op jit(solution)/shard_map/ppermute | solution.py:354
  71.6 12.1 %collective-permute-start.11 = (f32[32,2176]{1,0:T(8,128)S(1)}, f32[32,2176]{1,0:T(8,128)S(1)}, u32[]{:S(2)}, u32[]{:S(2)}) collective-permute-start(f32[32,2176]{1,0:T(8,128)S(1)} %slice_add_fusion.3), channel_id=1, source_target_pairs={{0,16},{4,20},{8,24},{12,28},{16,0},{20,4},{24,8},{28,12},{1,17},{... | collective-permute-start | bytes 835592 | tf_op jit(solution)/shard_map/ppermute | solution.py:354
  84.7 15.0 %collective-permute-start.14 = (f32[32,2304]{1,0:T(8,128)S(1)}, f32[32,2304]{1,0:T(8,128)S(1)}, u32[]{:S(2)}, u32[]{:S(2)}) collective-permute-start(f32[32,2304]{1,0:T(8,128)S(1)} %slice_add_fusion.1), channel_id=1, source_target_pairs={{0,16},{4,20},{8,24},{12,28},{16,0},{20,4},{24,8},{28,12},{1,17},{... | collective-permute-start | bytes 884744 | tf_op jit(solution)/shard_map/ppermute | solution.py:354
  87.3 11.2 %collective-permute-start.13 = (f32[32,2176]{1,0:T(8,128)S(1)}, f32[32,2176]{1,0:T(8,128)S(1)}, u32[]{:S(2)}, u32[]{:S(2)}) collective-permute-start(f32[32,2176]{1,0:T(8,128)S(1)} %add.71), channel_id=1, source_target_pairs={{0,8},{4,12},{8,0},{12,4},{16,24},{20,28},{24,16},{28,20},{1,9},{5... | collective-permute-start | bytes 835592 | tf_op jit(solution)/shard_map/ppermute | solution.py:354
  99.9 9.5 %collective-permute-start.15 = (f32[32,2304]{1,0:T(8,128)S(1)}, f32[32,2304]{1,0:T(8,128)S(1)}, u32[]{:S(2)}, u32[]{:S(2)}) collective-permute-start(f32[32,2304]{1,0:T(8,128)S(1)} %add.73), channel_id=1, source_target_pairs={{0,8},{4,12},{8,0},{12,4},{16,24},{20,28},{24,16},{28,20},{1,9},{5... | collective-permute-start | bytes 884744 | tf_op jit(solution)/shard_map/ppermute | solution.py:354
  122.8 16.6 %collective-permute-start.20 = (f32[520,128]{1,0:T(8,128)S(1)}, f32[520,128]{1,0:T(8,128)S(1)}, u32[]{:S(2)}, u32[]{:S(2)}) collective-permute-start(f32[520,128]{1,0:T(8,128)S(1)} %add.74.refs_0_), channel_id=1, source_target_pairs={{0,2},{1,3},{2,0},{3,1},{4,6},{5,7},{6,4},{7,5},{8,10},{9,11},{10,... | collective-permute-start | bytes 798728 | tf_op jit(solution)/shard_map/ppermute | solution.py:354
  126.3 13.1 %collective-permute-start.22 = (f32[520,128]{1,0:T(8,128)S(1)}, f32[520,128]{1,0:T(8,128)S(1)}, u32[]{:S(2)}, u32[]{:S(2)}) collective-permute-start(f32[520,128]{1,0:T(8,128)S(1)} %get-tuple-element.187), channel_id=1, source_target_pairs={{0,1},{1,0},{2,3},{3,2},{4,5},{5,4},{6,7},{7,6},{8,9},{9,8},{10,11... | collective-permute-start | bytes 798728 | tf_op jit(solution)/shard_map/ppermute | solution.py:354
  127.0 12.4 %collective-permute-start.21 = (f32[512,128]{1,0:T(8,128)S(1)}, f32[512,128]{1,0:T(8,128)S(1)}, u32[]{:S(2)}, u32[]{:S(2)}) collective-permute-start(f32[512,128]{1,0:T(8,128)S(1)} %add.75.refs_2_), channel_id=1, source_target_pairs={{0,1},{1,0},{2,3},{3,2},{4,5},{5,4},{6,7},{7,6},{8,9},{9,8},{10,11... | collective-permute-start | bytes 786440 | tf_op jit(solution)/shard_map/ppermute | solution.py:354
  128.5 10.9 %collective-permute-start.23 = (f32[512,128]{1,0:T(8,128)S(1)}, f32[512,128]{1,0:T(8,128)S(1)}, u32[]{:S(2)}, u32[]{:S(2)}) collective-permute-start(f32[512,128]{1,0:T(8,128)S(1)} %get-tuple-element.189), channel_id=1, source_target_pairs={{0,2},{1,3},{2,0},{3,1},{4,6},{5,7},{6,4},{7,5},{8,10},{9,11},{10,... | collective-permute-start | bytes 786440 | tf_op jit(solution)/shard_map/ppermute | solution.py:354
  142.6 10.2 %collective-permute-start.26 = (f32[64,2176]{1,0:T(8,128)S(1)}, f32[64,2176]{1,0:T(8,128)S(1)}, u32[]{:S(2)}, u32[]{:S(2)}) collective-permute-start(f32[64,2176]{1,0:T(8,128)S(1)} %get-tuple-element.196), channel_id=1, source_target_pairs={{0,4},{4,0},{8,12},{12,8},{16,20},{20,16},{24,28},{28,24},{1,5},{5... | collective-permute-start | bytes 1671176 | tf_op jit(solution)/shard_map/ppermute | solution.py:354
  142.7 10.1 %collective-permute-start.24 = (f32[520,128]{1,0:T(8,128)S(1)}, f32[520,128]{1,0:T(8,128)S(1)}, u32[]{:S(2)}, u32[]{:S(2)}) collective-permute-start(f32[520,128]{1,0:T(8,128)S(1)} %add.76.refs_1_), channel_id=1, source_target_pairs={{0,2},{1,3},{2,0},{3,1},{4,6},{5,7},{6,4},{7,5},{8,10},{9,11},{10,... | collective-permute-start | bytes 798728 | tf_op jit(solution)/shard_map/ppermute | solution.py:354
  156.6 9.3 %collective-permute-start.28 = (f32[64,2304]{1,0:T(8,128)S(1)}, f32[64,2304]{1,0:T(8,128)S(1)}, u32[]{:S(2)}, u32[]{:S(2)}) collective-permute-start(f32[64,2304]{1,0:T(8,128)S(1)} %get-tuple-element.207), channel_id=1, source_target_pairs={{0,4},{4,0},{8,12},{12,8},{16,20},{20,16},{24,28},{28,24},{1,5},{5... | collective-permute-start | bytes 1769480 | tf_op jit(solution)/shard_map/ppermute | solution.py:354
  166.0 14.7 %collective-permute-start.30 = (f32[32,2304]{1,0:T(8,128)S(1)}, f32[32,2304]{1,0:T(8,128)S(1)}, u32[]{:S(2)}, u32[]{:S(2)}) collective-permute-start(f32[32,2304]{1,0:T(8,128)S(1)} %slice.35), channel_id=1, source_target_pairs={{0,8},{4,12},{8,0},{12,4},{16,24},{20,28},{24,16},{28,20},{1,9},{5... | collective-permute-start | bytes 884744 | tf_op jit(solution)/shard_map/ppermute | solution.py:354
  167.4 12.1 %collective-permute-start.29 = (f32[32,2176]{1,0:T(8,128)S(1)}, f32[32,2176]{1,0:T(8,128)S(1)}, u32[]{:S(2)}, u32[]{:S(2)}) collective-permute-start(f32[32,2176]{1,0:T(8,128)S(1)} %slice_add_fusion.2), channel_id=1, source_target_pairs={{0,16},{4,20},{8,24},{12,28},{16,0},{20,4},{24,8},{28,12},{1,17},{... | collective-permute-start | bytes 835592 | tf_op jit(solution)/shard_map/ppermute | solution.py:354
  180.7 15.0 %collective-permute-start.32 = (f32[32,2304]{1,0:T(8,128)S(1)}, f32[32,2304]{1,0:T(8,128)S(1)}, u32[]{:S(2)}, u32[]{:S(2)}) collective-permute-start(f32[32,2304]{1,0:T(8,128)S(1)} %slice_add_fusion), channel_id=1, source_target_pairs={{0,16},{4,20},{8,24},{12,28},{16,0},{20,4},{24,8},{28,12},{1,17},{... | collective-permute-start | bytes 884744 | tf_op jit(solution)/shard_map/ppermute | solution.py:354
  183.1 11.2 %collective-permute-start.31 = (f32[32,2176]{1,0:T(8,128)S(1)}, f32[32,2176]{1,0:T(8,128)S(1)}, u32[]{:S(2)}, u32[]{:S(2)}) collective-permute-start(f32[32,2176]{1,0:T(8,128)S(1)} %add.81), channel_id=1, source_target_pairs={{0,8},{4,12},{8,0},{12,4},{16,24},{20,28},{24,16},{28,20},{1,9},{5... | collective-permute-start | bytes 835592 | tf_op jit(solution)/shard_map/ppermute | solution.py:354
  195.9 9.5 %collective-permute-start.33 = (f32[32,2304]{1,0:T(8,128)S(1)}, f32[32,2304]{1,0:T(8,128)S(1)}, u32[]{:S(2)}, u32[]{:S(2)}) collective-permute-start(f32[32,2304]{1,0:T(8,128)S(1)} %add.83), channel_id=1, source_target_pairs={{0,8},{4,12},{8,0},{12,4},{16,24},{20,28},{24,16},{28,20},{1,9},{5... | collective-permute-start | bytes 884744 | tf_op jit(solution)/shard_map/ppermute | solution.py:354
  213.1 9.7 %collective-permute-start.38 = (f32[8,256]{1,0:T(8,128)S(1)}, f32[8,256]{1,0:T(8,128)S(1)}, u32[]{:S(2)}, u32[]{:S(2)}) collective-permute-start(f32[8,256]{1,0:T(8,128)S(1)} %constant_dynamic-update-slice_fusion.8.s0), channel_id=1, source_target_pairs={{0,3},{1,2},{2,1},{3,0},{4,7},{5,6},{6,5},{7,4},{8,11},{9,10},{10,... | collective-permute-start | bytes 24584 | tf_op jit(solution)/shard_map/ppermute | solution.py:354
  (23 other events, 176.3 us)
where the time goes:
time: 231 us; the launch traced here: 230 us
  waiting for transfers between devices  105 us (45%)
  Pallas kernels  66.9 us (29%)
  starting transfers between devices  47.6 us (21%)
  local copies, waits for them, and re-layouts  8.67 us (4%)
    ppermute x39, waiting for transfers between devices, swap(): return lax.ppermute(x, axis, [(i, i ^ bit) for i in range(size)])  105 us
    ppermute x39, starting transfers between devices, swap(): return lax.ppermute(x, axis, [(i, i ^ bit) for i in range(size)])  47.6 us
    pallas_call x4, Pallas kernels, product(): call(functools.partial(product_kernel, not before, scaled), 'product', 4...  13.8 us
    pallas_call x2, Pallas kernels, second_solve(): call(second_kernel, 'second_solve', 6000000000, 20 * HALF * cols, out_sha...  12.2 us
    pallas_call x1, Pallas kernels, start(): call(start_kernel, 'start', 6 * rows * cols * RANK, 6 * rows * cols, out_...  10.8 us
    pallas_call x2, Pallas kernels, first_solve(): call(first_kernel, 'first_solve', 5000000000, 20 * HALF * cols, out_shape...  10.4 us
    unnamed x21, local copies, waits for them, and re-layouts  8.5 us
    pallas_call x1, Pallas kernels, weight_update(): call(weight_kernel, 'weight', 6 * rows * cols * RANK, 4 * rows * cols, ou...  7.39 us
  transfers between devices with their start and end apart: 39, of which 26 were waited for; matrix products, arithmetic and copies ran while one was open for 0% of the time, Pallas kernels for 13%

commit v1 on v0

--- a/solution.py
+++ b/solution.py
@@ -15,6 +15,7 @@
 PART = RANK // 8
 SUB = 8
 TILE = 256
+STEP = 512
 
 beta_mom = 0.95
 learn_rate = 0.05
@@ -127,22 +128,23 @@
         out_ref[pl.ds(pl.multiple_of((me ^ b) * PART, PART), PART), :] = block
 
 
-def start_kernel(momentum_ref, gradient_ref, basis_ref, high_ref, low_ref, up0, down0, up1, down1, bhigh_ref, blow_ref):
+def start_kernel(momentum_ref, gradient_ref, basis_ref, high_ref, low_ref, up0, down0, up1, down1, pair_ref):
     rows, cols = momentum_ref.shape
-    count = up0.shape[0] // HALF
+    count = up0.shape[0] // TILE
 
     def body(momentum, gradient, basis):
         step = pl.program_id(0)
 
         @pl.when(step == 0)
         def _():
-            bhigh_ref[...], blow_ref[...] = split(basis[...])
-
-        here = pl.ds(pl.multiple_of(step * HALF, HALF), HALF)
-        buffer = split(momentum[...] + gradient[...].astype(F32))
-        high_ref[here, :], low_ref[here, :] = buffer
-        part = dot3(buffer, (bhigh_ref[...], blow_ref[...]))
-        there = pl.ds(pl.multiple_of(lax.rem(step, count) * HALF, HALF), HALF)
+            pair_ref[:, :RANK], pair_ref[:, RANK:] = split(basis[...])
+
+        here = pl.ds(pl.multiple_of(step * TILE, TILE), TILE)
+        high, low = split(momentum[...] + gradient[...].astype(F32))
+        high_ref[here, :], low_ref[here, :] = high, low
+        both = dot(high, pair_ref[...])
+        part = (both[:, :RANK] + both[:, RANK:]) + dot(low, pair_ref[:, :RANK])
+        there = pl.ds(pl.multiple_of(lax.rem(step, count) * TILE, TILE), TILE)
 
         @pl.when(step < count)
         def _():
@@ -154,20 +156,21 @@
             down0[there, :] = part[:, :HALF]
             down1[there, :] = part[:, HALF:]
 
-    block = pl.BlockSpec((HALF, cols), lambda i: (i, 0))
+    block = pl.BlockSpec((TILE, cols), lambda i: (i, 0))
     pltpu.emit_pipeline(
-        body, grid=(rows // HALF,), in_specs=[block, block, pl.BlockSpec((cols, RANK), lambda i: (0, 0))],
+        body, grid=(rows // TILE,), in_specs=[block, block, pl.BlockSpec((cols, RANK), lambda i: (0, 0))],
     )(momentum_ref, gradient_ref, basis_ref)
 
 
 def start(*args):
     rows, cols = args[0].shape
-    return call(
+    high, low, *parts = call(
         start_kernel, "start", 6 * rows * cols * RANK, 6 * rows * cols,
         out_shape=[shaped(rows, cols, dtype=BF16)] * 2 + [shaped(rows // 2, HALF)] * 4,
         in_specs=[pl.BlockSpec(memory_space=pltpu.HBM)] * 3, out_specs=[VMEM] * 6,
-        scratch_shapes=[pltpu.VMEM((cols, RANK), BF16)] * 2,
+        scratch_shapes=[pltpu.VMEM((cols, 2 * RANK), BF16)],
     )(*(pltpu.with_memory_space_constraint(x, pltpu.HBM) for x in args))
+    return (*(pltpu.with_memory_space_constraint(x, pltpu.VMEM) for x in (high, low)), *parts)
 
 
 def left_kernel(high_ref, low_ref, factor_ref, *refs):
@@ -219,13 +222,11 @@
         give_ref[:, spot:spot + HALF] = gram[QUARTER:]
         spot += HALF
     step = 2 * TILE
-
-    @pl.loop(0, high_ref.shape[1] // step)
-    def _(c):
-        lanes = pl.ds(pl.multiple_of(c * step, step), step)
+    for c in range(high_ref.shape[1] // step):
+        lanes = pl.ds(c * step, step)
         both = dot(pair_ref[...], high_ref[:, lanes])
         part = (both[:HALF] + both[HALF:]) + dot(pair_ref[:HALF, :], low_ref[:, lanes])
-        lanes = pl.ds(pl.multiple_of(spot + c * step, HALF), step)
+        lanes = pl.ds(spot + c * step, step)
         keep_ref[:, lanes] = part[:QUARTER]
         give_ref[:, lanes] = part[QUARTER:]
 
@@ -316,25 +317,28 @@
     rows, cols = buffer[0].shape
     return call(
         momentum_kernel, "momentum", 2 * rows * cols * RANK, 4 * rows * cols,
-        out_shape=[shaped(rows, cols), shaped(rows, RANK)], grid=(cols // TILE,),
-        in_specs=[VMEM] * 7, out_specs=[pl.BlockSpec((rows, TILE), lambda i: (0, i)), VMEM],
+        out_shape=[shaped(rows, cols), shaped(rows, RANK)], grid=(cols // STEP,),
+        in_specs=[VMEM] * 7, out_specs=[pl.BlockSpec((rows, STEP), lambda i: (0, i)), VMEM],
         scratch_shapes=[pltpu.VMEM((rows, RANK), BF16)],
     )(*lefts, inverse, *pairs, *buffer)
 
 
-def weight_kernel(ortho_ref, s0, s1, s2, s3, pair0_ref, pair1_ref, factor0_ref, factor1_ref, weight_ref, out_ref, basis_ref, high_ref, low_ref):
+def weight_kernel(ortho_ref, s0, s1, s2, s3, pair0_ref, pair1_ref, factor0_ref, factor1_ref, weight_ref, out_ref, basis_ref, triple_ref):
     total = (s0[0:1, :] + s1[0:1, :]) + (s2[0:1, :] + s3[0:1, :])
     scale = 1.0 / jnp.sqrt(total / F32(D) + F32(1e-06))
     step, width = pl.program_id(0), out_ref.shape[1]
 
     @pl.when(step == 0)
     def _():
-        high_ref[...], low_ref[...] = split(ortho_ref[...] * (scale * F32(learn_rate * (D / RANK) ** 0.5)))
+        high, low = split(ortho_ref[...] * (scale * F32(learn_rate * (D / RANK) ** 0.5)))
+        triple_ref[:, :RANK] = high
+        triple_ref[:, RANK:2 * RANK] = low
+        triple_ref[:, 2 * RANK:] = high
 
     lanes = pl.ds(pl.multiple_of(step * width, width), width)
-    fhigh = jnp.concatenate([pair0_ref[:HALF, lanes], pair1_ref[:HALF, lanes]], axis=0)
-    flow = jnp.concatenate([pair0_ref[HALF:, lanes], pair1_ref[HALF:, lanes]], axis=0)
-    out_ref[...] = weight_ref[:, lanes] - dot3((high_ref[...], low_ref[...]), (fhigh, flow))
+    high = [pair0_ref[:HALF, lanes], pair1_ref[:HALF, lanes]]
+    factor = jnp.concatenate([*high, *high, pair0_ref[HALF:, lanes], pair1_ref[HALF:, lanes]], axis=0)
+    out_ref[...] = weight_ref[:, lanes] - dot(triple_ref[...], factor)
     basis_ref[:, :HALF] = factor0_ref[:, lanes].T * scale[:, :HALF]
     basis_ref[:, HALF:] = factor1_ref[:, lanes].T * scale[:, HALF:]
 
@@ -343,9 +347,9 @@
     rows, cols = weight.shape
     return call(
         weight_kernel, "weight", 6 * rows * cols * RANK, 4 * rows * cols,
-        out_shape=[shaped(rows, cols), shaped(cols, RANK)], grid=(cols // TILE,), in_specs=[VMEM] * 10,
-        out_specs=[pl.BlockSpec((rows, TILE), lambda i: (0, i)), pl.BlockSpec((TILE, RANK), lambda i: (i, 0))],
-        scratch_shapes=[pltpu.VMEM((rows, RANK), BF16)] * 2,
+        out_shape=[shaped(rows, cols), shaped(cols, RANK)], grid=(cols // STEP,), in_specs=[VMEM] * 10,
+        out_specs=[pl.BlockSpec((rows, STEP), lambda i: (0, i)), pl.BlockSpec((STEP, RANK), lambda i: (i, 0))],
+        scratch_shapes=[pltpu.VMEM((rows, 3 * RANK), BF16)],
     )(ortho, *squares, *pairs, *factors, weight)
 
 
@@ -370,26 +374,32 @@
 
         up0, down0 = up0 + got0[0], down0 + got0[1]
         got0 = swap(up0, "col", 2), swap(down0, "col", 1)
+        if not sweep:
+            got1 = swap(up1, "col", 1), swap(down1, "col", 2)
+            up0, down0, got0, up1, down1, got1 = together(up0, down0, got0, up1, down1, got1)
+            up1, down1 = up1 + got1[0], down1 + got1[1]
+            got1 = swap(up1, "col", 2), swap(down1, "col", 1)
+        else:
+            up1, down1 = left_product(buffer, split1, square1)
+            up0, down0, got0, up1, down1 = together(up0, down0, got0, up1, down1)
+            got1 = swap(up1, "col", 1), swap(down1, "col", 2)
+        keep0, give0, left0 = product(scaled, me, (), (up0, got0[0], down0, got0[1]), buffer)
+        up1, down1, got1, keep0, give0, left0 = together(up1, down1, got1, keep0, give0, left0)
+
+        core0 = swap(give0, "row", 1)
         if sweep:
-            up1, down1 = left_product(buffer, split1, square1)
-        got1 = swap(up1, "col", 1), swap(down1, "col", 2)
-        up0, down0, got0, up1, down1, got1 = together(up0, down0, got0, up1, down1, got1)
-
-        up1, down1 = up1 + got1[0], down1 + got1[1]
-        got1 = swap(up1, "col", 2), swap(down1, "col", 1)
-        keep0, give0, left0 = product(scaled, me, (), (up0, got0[0], down0, got0[1]), buffer)
-        core0 = swap(give0, "row", 1)
+            up1, down1 = up1 + got1[0], down1 + got1[1]
+            got1 = swap(up1, "col", 2), swap(down1, "col", 1)
         up1, down1, got1, keep0, core0, left0 = together(up1, down1, got1, keep0, core0, left0)
 
         part0 = keep0 + core0
         pair0 = swap(part0[PART:], "row", 2)
         keep1, give1, left1 = product(scaled, me, (left0,), (up1, got1[0], down1, got1[1]), buffer)
-        core1 = swap(give1, "row", 1)
-        part0, pair0, keep1, core1 = together(part0, pair0, keep1, core1)
+        part0, pair0, keep1, give1 = together(part0, pair0, keep1, give1)
 
         side0 = part0[:PART] + pair0
         cross0 = swap(side0, "row", 4)
-        part1 = keep1 + core1
+        part1 = keep1 + swap(give1, "row", 1)
         pair1 = swap(part1[PART:], "row", 2)
         side0, cross0, part1, pair1 = together(side0, cross0, part1, pair1)
 

time: 231 us -> 212 us (0.918)
  waiting for transfers between devices: 105 us -> 95 us
  Pallas kernels: 66.9 us -> 60.7 us
    ppermute x39, waiting for transfers between devices: 105 us -> 95 us  [swap(): return lax.ppermute(x, axis, [(i, i ^ bit) for i in range(size)])]
    pallas_call x4, Pallas kernels: 13.8 us -> 11.1 us  [product(): call(functools.partial(product_kernel, not before, scaled), 'product', 4...]
  transfers between devices with their start and end apart: 39 -> 39, of which waited for: 26 -> 29; matrix products, arithmetic and copies ran while one was open for 0% -> 0% of each run, Pallas kernels for 13% -> 19%
where the time goes in v1:
time: 212 us
  waiting for transfers between devices  95 us (45%)
  Pallas kernels  60.7 us (29%)
  starting transfers between devices  45.4 us (21%)
  local copies, waits for them, and re-layouts  8.67 us (4%)
    ppermute x39, waiting for transfers between devices, swap(): return lax.ppermute(x, axis, [(i, i ^ bit) for i in range(size)])  95 us
    ppermute x39, starting transfers between devices, swap(): return lax.ppermute(x, axis, [(i, i ^ bit) for i in range(size)])  45.4 us
    pallas_call x2, Pallas kernels, second_solve(): call(second_kernel, 'second_solve', 6000000000, 20 * HALF * cols, out_sha...  12.5 us
    pallas_call x4, Pallas kernels, product(): call(functools.partial(product_kernel, not before, scaled), 'product', 4...  11.1 us
    pallas_call x2, Pallas kernels, first_solve(): call(first_kernel, 'first_solve', 5000000000, 20 * HALF * cols, out_shape...  10.4 us
    pallas_call x1, Pallas kernels, start(): call(start_kernel, 'start', 6 * rows * cols * RANK, 6 * rows * cols, out_...  9.14 us
    unnamed x21, local copies, waits for them, and re-layouts  8.5 us
    pallas_call x2, Pallas kernels, left_product(): call(left_kernel, 'left', 4 * rows * cols * RANK, 4 * rows * cols, out_sh...  6.29 us
  transfers between devices with their start and end apart: 39, of which 29 were waited for; matrix products, arithmetic and copies ran while one was open for 0% of the time, Pallas kernels for 19%

profile of v1, /device:TPU:0, one launch (start us, length us, event | category | flops | bytes accessed | tf_op | source)
XLA Modules:
  0.0 211.5 jit_solution(5396270439193409930)
XLA Ops:
  0.6 9.1 %start.1 = (bf16[1024,2048]{1,0:T(8,128)(2,1)S(1)}, bf16[1024,2048]{1,0:T(8,128)(2,1)S(1)}, f32[512,128]{1,0:T(8,128)S(1)}, f32[512,128]{1,0:T(8,128)S(1)}, f32[...) custom-call(f32[1024,2048]{1,0:T(8,128)} %bitcast.6, bf16[1024,2048]{1,0:T(8,128)(2,1)} %bitcast.7, f32[2048,256]{1,0:T(8,128)} %basis_ref.1), custom_call_target="tpu_custom_call" | custom-call | flops 3221225472 | bytes 12582912 | tf_op jit(solution)/shard_map/start/pallas_call | solution.py:167
  13.8 2.9 %collective-permute-start = (f32[512,128]{1,0:T(8,128)S(1)}, f32[512,128]{1,0:T(8,128)S(1)}, u32[]{:S(2)}, u32[]{:S(2)}) collective-permute-start(f32[512,128]{1,0:T(8,128)S(1)} %get-tuple-element.139), channel_id=1, source_target_pairs={{0,1},{1,0},{2,3},{3,2},{4,5},{5,4},{6,7},{7,6},{8,9},{9,8},{10,11... | collective-permute-start | bytes 786440 | tf_op jit(solution)/shard_map/ppermute | solution.py:358
  18.3 4.8 %collective-permute-done = f32[512,128]{1,0:T(8,128)S(1)} collective-permute-done((f32[512,128]{1,0:T(8,128)S(1)}, f32[512,128]{1,0:T(8,128)S(1)}, u32[]{:S(2)}, u32[]{:S(2)}) %collective-permute-start) | collective-permute-done | bytes 262176 | tf_op jit(solution)/shard_map/ppermute | solution.py:358
  28.8 5.1 %collective-permute-done.3.refs_3_ = f32[512,128]{1,0:T(8,128)S(1)} collective-permute-done((f32[512,128]{1,0:T(8,128)S(1)}, f32[512,128]{1,0:T(8,128)S(1)}, u32[]{:S(2)}, u32[]{:S(2)}) %collective-permute-start.3) | collective-permute-done | bytes 262176 | tf_op jit(solution)/shard_map/ppermute | solution.py:358
  34.3 2.8 %collective-permute-done.4 = f32[512,128]{1,0:T(8,128)S(1)} collective-permute-done((f32[512,128]{1,0:T(8,128)S(1)}, f32[512,128]{1,0:T(8,128)S(1)}, u32[]{:S(2)}, u32[]{:S(2)}) %collective-permute-start.4) | collective-permute-done | bytes 262176 | tf_op jit(solution)/shard_map/ppermute | solution.py:358
  51.2 3.5 %product.5 = (f32[64,2304]{1,0:T(8,128)S(1)}, f32[64,2304]{1,0:T(8,128)S(1)}, f32[1024,128]{1,0:T(8,128)}) custom-call(s32[1]{0:T(128)} %bitcast.2.me_ref, f32[1024,128]{1,0:T(8,128)S(1)} %get-tuple-element.165.refs_0_, f32[512,128]{1,0:T(8,128)S(1)} %add.65.refs_1_, f32[512,128]{1,0:T(8,128)S(1)} %collective-permute-done.6.refs_2_, ...), custom_call_target="tpu_custom_call" | custom-call | flops 2415919104 | bytes 9437184 | tf_op jit(solution)/shard_map/product/pallas_call | solution.py:237
  54.7 3.7 %collective-permute-done.9 = f32[32,2176]{1,0:T(8,128)S(1)} collective-permute-done((f32[32,2176]{1,0:T(8,128)S(1)}, f32[32,2176]{1,0:T(8,128)S(1)}, u32[]{:S(2)}, u32[]{:S(2)}) %collective-permute-start.9) | collective-permute-done | bytes 278560 | tf_op jit(solution)/shard_map/ppermute | solution.py:358
  64.8 9.9 %collective-permute-done.10 = f32[32,2176]{1,0:T(8,128)S(1)} collective-permute-done((f32[32,2176]{1,0:T(8,128)S(1)}, f32[32,2176]{1,0:T(8,128)S(1)}, u32[]{:S(2)}, u32[]{:S(2)}) %collective-permute-start.10) | collective-permute-done | bytes 278560 | tf_op jit(solution)/shard_map/ppermute | solution.py:358
  80.8 9.2 %collective-permute-done.13 = f32[32,2176]{1,0:T(8,128)S(1)} collective-permute-done((f32[32,2176]{1,0:T(8,128)S(1)}, f32[32,2176]{1,0:T(8,128)S(1)}, u32[]{:S(2)}, u32[]{:S(2)}) %collective-permute-start.13) | collective-permute-done | bytes 278560 | tf_op jit(solution)/shard_map/ppermute | solution.py:358
  93.1 5.6 %first_solve.2 = (f32[128,128]{1,0:T(8,128)S(1)}, f32[128,2048]{1,0:T(8,128)S(1)}, f32[128,2048]{1,0:T(8,128)}, bf16[256,2048]{1,0:T(8,128)(2,1)S(1)}, f32[8,128]{1,0:T(8,128)S(1)}) custom-call(s32[1]{0:T(128)} %bitcast.2.me_ref, f32[64,2176]{1,0:T(8,128)S(1)} %constant_dynamic-update-slice_fusion.mine_ref, f32[64,2176]{1,0:T(8,128)S(1)} %collective-permute-done.16.other_ref), custom_call_target="tpu_custom_call" | custom-call | flops 5000000000 | bytes 5242880 | tf_op jit(solution)/shard_map/first_solve/pallas_call | solution.py:268
  100.9 3.1 %left.2 = (f32[520,128]{1,0:T(8,128)S(1)}, f32[512,128]{1,0:T(8,128)S(1)}) custom-call(bf16[1024,2048]{1,0:T(8,128)(2,1)S(1)} %copy-done.2, bf16[1024,2048]{1,0:T(8,128)(2,1)S(1)} %copy-done.5, bf16[256,2048]{1,0:T(8,128)(2,1)S(1)} %get-tuple-element.188.factor_ref, f32[8,128]{1,0:T(8,128)S(1)} %get-tuple-element.189.refs_0_), custom_call_target="tpu_custom_call" | custom-call | flops 2147483648 | bytes 8388608 | tf_op jit(solution)/shard_map/left/pallas_call | solution.py:194
  105.2 6.6 %second_solve.2 = (f32[256,256]{1,0:T(8,128)}, f32[128,2048]{1,0:T(8,128)}, bf16[256,2048]{1,0:T(8,128)(2,1)S(1)}, f32[8,128]{1,0:T(8,128)S(1)}) custom-call(s32[1]{0:T(128)} %bitcast.2.me_ref, f32[64,2304]{1,0:T(8,128)S(1)} %constant_dynamic-update-slice_fusion.2.mine_ref, f32[64,2304]{1,0:T(8,128)S(1)} %collective-permute-done.19.other_ref, ...), custom_call_target="tpu_custom_call" | custom-call | flops 6000000000 | bytes 5242880 | tf_op jit(solution)/shard_map/second_solve/pallas_call | solution.py:292
  115.2 3.2 %left.3 = (f32[520,128]{1,0:T(8,128)S(1)}, f32[512,128]{1,0:T(8,128)S(1)}) custom-call(bf16[1024,2048]{1,0:T(8,128)(2,1)S(1)} %copy-done.2, bf16[1024,2048]{1,0:T(8,128)(2,1)S(1)} %copy-done.5, bf16[256,2048]{1,0:T(8,128)(2,1)S(1)} %get-tuple-element.202.factor_ref, f32[8,128]{1,0:T(8,128)S(1)} %get-tuple-element.203.refs_0_), custom_call_target="tpu_custom_call" | custom-call | flops 2147483648 | bytes 8388608 | tf_op jit(solution)/shard_map/left/pallas_call | solution.py:194
  118.4 3.3 %collective-permute-done.21.refs_3_ = f32[512,128]{1,0:T(8,128)S(1)} collective-permute-done((f32[512,128]{1,0:T(8,128)S(1)}, f32[512,128]{1,0:T(8,128)S(1)}, u32[]{:S(2)}, u32[]{:S(2)}) %collective-permute-start.21) | collective-permute-done | bytes 262176 | tf_op jit(solution)/shard_map/ppermute | solution.py:358
  125.6 3.4 %collective-permute-done.23 = f32[512,128]{1,0:T(8,128)S(1)} collective-permute-done((f32[512,128]{1,0:T(8,128)S(1)}, f32[512,128]{1,0:T(8,128)S(1)}, u32[]{:S(2)}, u32[]{:S(2)}) %collective-permute-start.23) | collective-permute-done | bytes 262176 | tf_op jit(solution)/shard_map/ppermute | solution.py:358
  130.9 7.3 %collective-permute-done.25.refs_4_ = f32[512,128]{1,0:T(8,128)S(1)} collective-permute-done((f32[512,128]{1,0:T(8,128)S(1)}, f32[512,128]{1,0:T(8,128)S(1)}, u32[]{:S(2)}, u32[]{:S(2)}) %collective-permute-start.25) | collective-permute-done | bytes 262176 | tf_op jit(solution)/shard_map/ppermute | solution.py:358
  139.6 2.8 %product.7 = (f32[64,2304]{1,0:T(8,128)S(1)}, f32[64,2304]{1,0:T(8,128)S(1)}, f32[1024,128]{1,0:T(8,128)S(1)}) custom-call(s32[1]{0:T(128)} %bitcast.2.me_ref, f32[1024,128]{1,0:T(8,128)S(1)} %get-tuple-element.222.refs_0_.left0_ref, f32[520,128]{1,0:T(8,128)S(1)} %add.76.refs_1_, f32[520,128]{1,0:T(8,128)S(1)} %collective-permute-done.24.refs_2_, ...), custom_call_target="tpu_custom_call" | custom-call | flops 2415919104 | bytes 9437184 | tf_op jit(solution)/shard_map/product/pallas_call | solution.py:237
  142.5 3.9 %collective-permute-done.27 = f32[32,2176]{1,0:T(8,128)S(1)} collective-permute-done((f32[32,2176]{1,0:T(8,128)S(1)}, f32[32,2176]{1,0:T(8,128)S(1)}, u32[]{:S(2)}, u32[]{:S(2)}) %collective-permute-start.27) | collective-permute-done | bytes 278560 | tf_op jit(solution)/shard_map/ppermute | solution.py:358
  151.8 10.6 %collective-permute-done.28 = f32[32,2176]{1,0:T(8,128)S(1)} collective-permute-done((f32[32,2176]{1,0:T(8,128)S(1)}, f32[32,2176]{1,0:T(8,128)S(1)}, u32[]{:S(2)}, u32[]{:S(2)}) %collective-permute-start.28) | collective-permute-done | bytes 278560 | tf_op jit(solution)/shard_map/ppermute | solution.py:358
  168.5 9.2 %collective-permute-done.31 = f32[32,2176]{1,0:T(8,128)S(1)} collective-permute-done((f32[32,2176]{1,0:T(8,128)S(1)}, f32[32,2176]{1,0:T(8,128)S(1)}, u32[]{:S(2)}, u32[]{:S(2)}) %collective-permute-start.31) | collective-permute-done | bytes 278560 | tf_op jit(solution)/shard_map/ppermute | solution.py:358
  181.2 4.8 %first_solve.3 = (f32[128,128]{1,0:T(8,128)S(1)}, f32[128,2048]{1,0:T(8,128)S(1)}, f32[128,2048]{1,0:T(8,128)S(1)}, bf16[256,2048]{1,0:T(8,128)(2,1)S(1)}, f32[8,128]{1,0:T(8,128)S(1)}) custom-call(s32[1]{0:T(128)} %bitcast.2.me_ref, f32[64,2176]{1,0:T(8,128)S(1)} %constant_dynamic-update-slice_fusion.4.mine_ref, ...), custom_call_target="tpu_custom_call" | custom-call | flops 5000000000 | bytes 5242880 | tf_op jit(solution)/shard_map/first_solve/pallas_call | solution.py:268
  190.9 5.9 %second_solve.3 = (f32[256,256]{1,0:T(8,128)S(1)}, f32[128,2048]{1,0:T(8,128)S(1)}, bf16[256,2048]{1,0:T(8,128)(2,1)S(1)}, f32[8,128]{1,0:T(8,128)S(1)}) custom-call(s32[1]{0:T(128)} %bitcast.2.me_ref, f32[64,2304]{1,0:T(8,128)S(1)} %constant_dynamic-update-slice_fusion.6.mine_ref, f32[64,2304]{1,0:T(8,128)S(1)} %collective-permute-done.35.other_ref, ...), custom_call_target="tpu_custom_call" | custom-call | flops 6000000000 | bytes 5242880 | tf_op jit(solution)/shard_map/second_solve/pallas_call | solution.py:292
  200.3 5.0 %momentum.1 = (f32[1024,2048]{1,0:T(8,128)}, f32[1024,256]{1,0:T(8,128)S(1)}) custom-call(f32[1024,128]{1,0:T(8,128)S(1)} %get-tuple-element.222.refs_0_.left0_ref, f32[1024,128]{1,0:T(8,128)S(1)} %get-tuple-element.227.left1_ref, f32[256,256]{1,0:T(8,128)S(1)} %get-tuple-element.252.inverse_ref, bf16[256,2048]{1,0:T(8,128)(2,1)S(1)} %get-tuple-element.253.pair0_ref, ...), custom_call_target="tpu_custom_call" | custom-call | flops 1073741824 | bytes 8388608 | tf_op jit(solution)/shard_map/momentum/pallas_call | solution.py:318
  205.3 6.2 %weight.1 = (f32[1024,2048]{1,0:T(8,128)}, f32[2048,256]{1,0:T(8,128)}) custom-call(f32[1024,256]{1,0:T(8,128)S(1)} %get-tuple-element.256.ortho_ref, f32[8,256]{1,0:T(8,128)S(1)} %constant_dynamic-update-slice_fusion.8.s0, f32[8,256]{1,0:T(8,128)S(1)} %collective-permute-done.36.s1, f32[8,256]{1,0:T(8,128)S(1)} %collective-permute-done.37.s2, ...), custom_call_target="tpu_custom_call" | custom-call | flops 3221225472 | bytes 8388608 | tf_op jit(solution)/shard_map/weight/pallas_call | solution.py:348
  (118 shorter events, 78.6 us)
Async XLA Ops:
  13.8 9.2 %collective-permute-start = (f32[512,128]{1,0:T(8,128)S(1)}, f32[512,128]{1,0:T(8,128)S(1)}, u32[]{:S(2)}, u32[]{:S(2)}) collective-permute-start(f32[512,128]{1,0:T(8,128)S(1)} %get-tuple-element.139), channel_id=1, source_target_pairs={{0,1},{1,0},{2,3},{3,2},{4,5},{5,4},{6,7},{7,6},{8,9},{9,8},{10,11... | collective-permute-start | bytes 786440 | tf_op jit(solution)/shard_map/ppermute | solution.py:358
  24.5 9.3 %collective-permute-start.3 = (f32[512,128]{1,0:T(8,128)S(1)}, f32[512,128]{1,0:T(8,128)S(1)}, u32[]{:S(2)}, u32[]{:S(2)}) collective-permute-start(f32[512,128]{1,0:T(8,128)S(1)} %add.64.refs_2_), channel_id=1, source_target_pairs={{0,1},{1,0},{2,3},{3,2},{4,5},{5,4},{6,7},{7,6},{8,9},{9,8},{10,11... | collective-permute-start | bytes 786440 | tf_op jit(solution)/shard_map/ppermute | solution.py:358
  25.0 9.3 %collective-permute-start.2 = (f32[512,128]{1,0:T(8,128)S(1)}, f32[512,128]{1,0:T(8,128)S(1)}, u32[]{:S(2)}, u32[]{:S(2)}) collective-permute-start(f32[512,128]{1,0:T(8,128)S(1)} %add.63.refs_0_), channel_id=1, source_target_pairs={{0,2},{1,3},{2,0},{3,1},{4,6},{5,7},{6,4},{7,5},{8,10},{9,11},{10,... | collective-permute-start | bytes 786440 | tf_op jit(solution)/shard_map/ppermute | solution.py:358
  26.8 10.3 %collective-permute-start.4 = (f32[512,128]{1,0:T(8,128)S(1)}, f32[512,128]{1,0:T(8,128)S(1)}, u32[]{:S(2)}, u32[]{:S(2)}) collective-permute-start(f32[512,128]{1,0:T(8,128)S(1)} %get-tuple-element.145), channel_id=1, source_target_pairs={{0,1},{1,0},{2,3},{3,2},{4,5},{5,4},{6,7},{7,6},{8,9},{9,8},{10,11... | collective-permute-start | bytes 786440 | tf_op jit(solution)/shard_map/ppermute | solution.py:358
  28.3 9.3 %collective-permute-start.5 = (f32[512,128]{1,0:T(8,128)S(1)}, f32[512,128]{1,0:T(8,128)S(1)}, u32[]{:S(2)}, u32[]{:S(2)}) collective-permute-start(f32[512,128]{1,0:T(8,128)S(1)} %get-tuple-element.147), channel_id=1, source_target_pairs={{0,2},{1,3},{2,0},{3,1},{4,6},{5,7},{6,4},{7,5},{8,10},{9,11},{10,... | collective-permute-start | bytes 786440 | tf_op jit(solution)/shard_map/ppermute | solution.py:358
  37.6 9.9 %collective-permute-start.7 = (f32[512,128]{1,0:T(8,128)S(1)}, f32[512,128]{1,0:T(8,128)S(1)}, u32[]{:S(2)}, u32[]{:S(2)}) collective-permute-start(f32[512,128]{1,0:T(8,128)S(1)} %add.66.refs_3_), channel_id=1, source_target_pairs={{0,1},{1,0},{2,3},{3,2},{4,5},{5,4},{6,7},{7,6},{8,9},{9,8},{10,11... | collective-permute-start | bytes 786440 | tf_op jit(solution)/shard_map/ppermute | solution.py:358
  39.1 8.4 %collective-permute-start.6 = (f32[512,128]{1,0:T(8,128)S(1)}, f32[512,128]{1,0:T(8,128)S(1)}, u32[]{:S(2)}, u32[]{:S(2)}) collective-permute-start(f32[512,128]{1,0:T(8,128)S(1)} %add.65.refs_1_), channel_id=1, source_target_pairs={{0,2},{1,3},{2,0},{3,1},{4,6},{5,7},{6,4},{7,5},{8,10},{9,11},{10,... | collective-permute-start | bytes 786440 | tf_op jit(solution)/shard_map/ppermute | solution.py:358
  49.6 8.8 %collective-permute-start.9 = (f32[32,2176]{1,0:T(8,128)S(1)}, f32[32,2176]{1,0:T(8,128)S(1)}, u32[]{:S(2)}, u32[]{:S(2)}) collective-permute-start(f32[32,2176]{1,0:T(8,128)S(1)} %slice.32), channel_id=1, source_target_pairs={{0,8},{4,12},{8,0},{12,4},{16,24},{20,28},{24,16},{28,20},{1,9},{5... | collective-permute-start | bytes 835592 | tf_op jit(solution)/shard_map/ppermute | solution.py:358
  60.4 15.1 %collective-permute-start.12 = (f32[32,2304]{1,0:T(8,128)S(1)}, f32[32,2304]{1,0:T(8,128)S(1)}, u32[]{:S(2)}, u32[]{:S(2)}) collective-permute-start(f32[32,2304]{1,0:T(8,128)S(1)} %slice.33), channel_id=1, source_target_pairs={{0,8},{4,12},{8,0},{12,4},{16,24},{20,28},{24,16},{28,20},{1,9},{5... | collective-permute-start | bytes 884744 | tf_op jit(solution)/shard_map/ppermute | solution.py:358
  62.1 12.6 %collective-permute-start.10 = (f32[32,2176]{1,0:T(8,128)S(1)}, f32[32,2176]{1,0:T(8,128)S(1)}, u32[]{:S(2)}, u32[]{:S(2)}) collective-permute-start(f32[32,2176]{1,0:T(8,128)S(1)} %slice_add_fusion.3), channel_id=1, source_target_pairs={{0,16},{4,20},{8,24},{12,28},{16,0},{20,4},{24,8},{28,12},{1,17},{... | collective-permute-start | bytes 835592 | tf_op jit(solution)/shard_map/ppermute | solution.py:358
  75.6 15.5 %collective-permute-start.14 = (f32[32,2304]{1,0:T(8,128)S(1)}, f32[32,2304]{1,0:T(8,128)S(1)}, u32[]{:S(2)}, u32[]{:S(2)}) collective-permute-start(f32[32,2304]{1,0:T(8,128)S(1)} %slice_add_fusion.1), channel_id=1, source_target_pairs={{0,16},{4,20},{8,24},{12,28},{16,0},{20,4},{24,8},{28,12},{1,17},{... | collective-permute-start | bytes 884744 | tf_op jit(solution)/shard_map/ppermute | solution.py:358
  78.2 11.7 %collective-permute-start.13 = (f32[32,2176]{1,0:T(8,128)S(1)}, f32[32,2176]{1,0:T(8,128)S(1)}, u32[]{:S(2)}, u32[]{:S(2)}) collective-permute-start(f32[32,2176]{1,0:T(8,128)S(1)} %add.71), channel_id=1, source_target_pairs={{0,8},{4,12},{8,0},{12,4},{16,24},{20,28},{24,16},{28,20},{1,9},{5... | collective-permute-start | bytes 835592 | tf_op jit(solution)/shard_map/ppermute | solution.py:358
  91.3 9.5 %collective-permute-start.15 = (f32[32,2304]{1,0:T(8,128)S(1)}, f32[32,2304]{1,0:T(8,128)S(1)}, u32[]{:S(2)}, u32[]{:S(2)}) collective-permute-start(f32[32,2304]{1,0:T(8,128)S(1)} %add.73), channel_id=1, source_target_pairs={{0,8},{4,12},{8,0},{12,4},{16,24},{20,28},{24,16},{28,20},{1,9},{5... | collective-permute-start | bytes 884744 | tf_op jit(solution)/shard_map/ppermute | solution.py:358
  104.0 8.6 %collective-permute-start.18 = (f32[512,128]{1,0:T(8,128)S(1)}, f32[512,128]{1,0:T(8,128)S(1)}, u32[]{:S(2)}, u32[]{:S(2)}) collective-permute-start(f32[512,128]{1,0:T(8,128)S(1)} %get-tuple-element.200), channel_id=1, source_target_pairs={{0,2},{1,3},{2,0},{3,1},{4,6},{5,7},{6,4},{7,5},{8,10},{9,11},{10,... | collective-permute-start | bytes 786440 | tf_op jit(solution)/shard_map/ppermute | solution.py:358
  113.0 8.8 %collective-permute-start.20 = (f32[520,128]{1,0:T(8,128)S(1)}, f32[520,128]{1,0:T(8,128)S(1)}, u32[]{:S(2)}, u32[]{:S(2)}) collective-permute-start(f32[520,128]{1,0:T(8,128)S(1)} %add.74.refs_0_), channel_id=1, source_target_pairs={{0,2},{1,3},{2,0},{3,1},{4,6},{5,7},{6,4},{7,5},{8,10},{9,11},{10,... | collective-permute-start | bytes 798728 | tf_op jit(solution)/shard_map/ppermute | solution.py:358
  129.0 9.2 %collective-permute-start.26 = (f32[64,2176]{1,0:T(8,128)S(1)}, f32[64,2176]{1,0:T(8,128)S(1)}, u32[]{:S(2)}, u32[]{:S(2)}) collective-permute-start(f32[64,2176]{1,0:T(8,128)S(1)} %get-tuple-element.220), channel_id=1, source_target_pairs={{0,4},{4,0},{8,12},{12,8},{16,20},{20,16},{24,28},{28,24},{1,5},{5... | collective-permute-start | bytes 1671176 | tf_op jit(solution)/shard_map/ppermute | solution.py:358
  129.0 9.1 %collective-permute-start.24 = (f32[520,128]{1,0:T(8,128)S(1)}, f32[520,128]{1,0:T(8,128)S(1)}, u32[]{:S(2)}, u32[]{:S(2)}) collective-permute-start(f32[520,128]{1,0:T(8,128)S(1)} %add.76.refs_1_), channel_id=1, source_target_pairs={{0,2},{1,3},{2,0},{3,1},{4,6},{5,7},{6,4},{7,5},{8,10},{9,11},{10,... | collective-permute-start | bytes 798728 | tf_op jit(solution)/shard_map/ppermute | solution.py:358
  129.6 8.5 %collective-permute-start.25 = (f32[512,128]{1,0:T(8,128)S(1)}, f32[512,128]{1,0:T(8,128)S(1)}, u32[]{:S(2)}, u32[]{:S(2)}) collective-permute-start(f32[512,128]{1,0:T(8,128)S(1)} %add.77.refs_3_), channel_id=1, source_target_pairs={{0,1},{1,0},{2,3},{3,2},{4,5},{5,4},{6,7},{7,6},{8,9},{9,8},{10,11... | collective-permute-start | bytes 786440 | tf_op jit(solution)/shard_map/ppermute | solution.py:358
  148.5 15.1 %collective-permute-start.30 = (f32[32,2304]{1,0:T(8,128)S(1)}, f32[32,2304]{1,0:T(8,128)S(1)}, u32[]{:S(2)}, u32[]{:S(2)}) collective-permute-start(f32[32,2304]{1,0:T(8,128)S(1)} %slice.35), channel_id=1, source_target_pairs={{0,8},{4,12},{8,0},{12,4},{16,24},{20,28},{24,16},{28,20},{1,9},{5... | collective-permute-start | bytes 884744 | tf_op jit(solution)/shard_map/ppermute | solution.py:358
  149.9 12.5 %collective-permute-start.28 = (f32[32,2176]{1,0:T(8,128)S(1)}, f32[32,2176]{1,0:T(8,128)S(1)}, u32[]{:S(2)}, u32[]{:S(2)}) collective-permute-start(f32[32,2176]{1,0:T(8,128)S(1)} %slice_add_fusion.2), channel_id=1, source_target_pairs={{0,16},{4,20},{8,24},{12,28},{16,0},{20,4},{24,8},{28,12},{1,17},{... | collective-permute-start | bytes 835592 | tf_op jit(solution)/shard_map/ppermute | solution.py:358
  163.6 15.5 %collective-permute-start.32 = (f32[32,2304]{1,0:T(8,128)S(1)}, f32[32,2304]{1,0:T(8,128)S(1)}, u32[]{:S(2)}, u32[]{:S(2)}) collective-permute-start(f32[32,2304]{1,0:T(8,128)S(1)} %slice_add_fusion), channel_id=1, source_target_pairs={{0,16},{4,20},{8,24},{12,28},{16,0},{20,4},{24,8},{28,12},{1,17},{... | collective-permute-start | bytes 884744 | tf_op jit(solution)/shard_map/ppermute | solution.py:358
  166.0 11.7 %collective-permute-start.31 = (f32[32,2176]{1,0:T(8,128)S(1)}, f32[32,2176]{1,0:T(8,128)S(1)}, u32[]{:S(2)}, u32[]{:S(2)}) collective-permute-start(f32[32,2176]{1,0:T(8,128)S(1)} %add.81), channel_id=1, source_target_pairs={{0,8},{4,12},{8,0},{12,4},{16,24},{20,28},{24,16},{28,20},{1,9},{5... | collective-permute-start | bytes 835592 | tf_op jit(solution)/shard_map/ppermute | solution.py:358
  179.3 9.5 %collective-permute-start.33 = (f32[32,2304]{1,0:T(8,128)S(1)}, f32[32,2304]{1,0:T(8,128)S(1)}, u32[]{:S(2)}, u32[]{:S(2)}) collective-permute-start(f32[32,2304]{1,0:T(8,128)S(1)} %add.83), channel_id=1, source_target_pairs={{0,8},{4,12},{8,0},{12,4},{16,24},{20,28},{24,16},{28,20},{1,9},{5... | collective-permute-start | bytes 884744 | tf_op jit(solution)/shard_map/ppermute | solution.py:358
  196.8 8.5 %collective-permute-start.38 = (f32[8,256]{1,0:T(8,128)S(1)}, f32[8,256]{1,0:T(8,128)S(1)}, u32[]{:S(2)}, u32[]{:S(2)}) collective-permute-start(f32[8,256]{1,0:T(8,128)S(1)} %constant_dynamic-update-slice_fusion.8.s0), channel_id=1, source_target_pairs={{0,3},{1,2},{2,1},{3,0},{4,7},{5,6},{6,5},{7,4},{8,11},{9,10},{10,... | collective-permute-start | bytes 24584 | tf_op jit(solution)/shard_map/ppermute | solution.py:358
  (23 other events, 142.0 us)

commit v2 on v1

--- a/solution.py
+++ b/solution.py
@@ -56,6 +56,7 @@
 
 
 VMEM = pl.BlockSpec(memory_space=pltpu.VMEM)
+HBM = pl.BlockSpec(memory_space=pltpu.HBM)
 SMEM = pl.BlockSpec(memory_space=pltpu.SMEM)
 
 
@@ -132,16 +133,15 @@
     rows, cols = momentum_ref.shape
     count = up0.shape[0] // TILE
 
-    def body(momentum, gradient, basis):
+    def body(momentum, gradient, basis, high_out, low_out):
         step = pl.program_id(0)
 
         @pl.when(step == 0)
         def _():
             pair_ref[:, :RANK], pair_ref[:, RANK:] = split(basis[...])
 
-        here = pl.ds(pl.multiple_of(step * TILE, TILE), TILE)
         high, low = split(momentum[...] + gradient[...].astype(F32))
-        high_ref[here, :], low_ref[here, :] = high, low
+        high_out[...], low_out[...] = high, low
         both = dot(high, pair_ref[...])
         part = (both[:, :RANK] + both[:, RANK:]) + dot(low, pair_ref[:, :RANK])
         there = pl.ds(pl.multiple_of(lax.rem(step, count) * TILE, TILE), TILE)
@@ -158,19 +158,23 @@
 
     block = pl.BlockSpec((TILE, cols), lambda i: (i, 0))
     pltpu.emit_pipeline(
-        body, grid=(rows // TILE,), in_specs=[block, block, pl.BlockSpec((cols, RANK), lambda i: (0, 0))],
-    )(momentum_ref, gradient_ref, basis_ref)
+        body, grid=(rows // TILE,), in_specs=[block, block, pl.BlockSpec((cols, RANK), lambda i: (0, 0))], out_specs=[block] * 2,
+    )(momentum_ref, gradient_ref, basis_ref, high_ref, low_ref)
+
+
+def in_hbm(*arrays):
+    return tuple(pltpu.with_memory_space_constraint(x, pltpu.HBM) for x in arrays)
 
 
 def start(*args):
     rows, cols = args[0].shape
     high, low, *parts = call(
-        start_kernel, "start", 6 * rows * cols * RANK, 6 * rows * cols,
-        out_shape=[shaped(rows, cols, dtype=BF16)] * 2 + [shaped(rows // 2, HALF)] * 4,
-        in_specs=[pl.BlockSpec(memory_space=pltpu.HBM)] * 3, out_specs=[VMEM] * 6,
+        start_kernel, "start", 6 * rows * cols * RANK, 10 * rows * cols,
+        out_shape=[pltpu.HBM((rows, cols), BF16)] * 2 + [shaped(rows // 2, HALF)] * 4,
+        in_specs=[HBM] * 3, out_specs=[HBM] * 2 + [VMEM] * 4,
         scratch_shapes=[pltpu.VMEM((cols, 2 * RANK), BF16)],
-    )(*(pltpu.with_memory_space_constraint(x, pltpu.HBM) for x in args))
-    return (*(pltpu.with_memory_space_constraint(x, pltpu.VMEM) for x in (high, low)), *parts)
+    )(*in_hbm(*args))
+    return high, low, *parts
 
 
 def left_kernel(high_ref, low_ref, factor_ref, *refs):
@@ -221,14 +225,30 @@
         keep_ref[:, spot:spot + HALF] = gram[:QUARTER]
         give_ref[:, spot:spot + HALF] = gram[QUARTER:]
         spot += HALF
-    step = 2 * TILE
-    for c in range(high_ref.shape[1] // step):
-        lanes = pl.ds(c * step, step)
-        both = dot(pair_ref[...], high_ref[:, lanes])
-        part = (both[:HALF] + both[HALF:]) + dot(pair_ref[:HALF, :], low_ref[:, lanes])
-        lanes = pl.ds(spot + c * step, step)
+    cols = high_ref.shape[1]
+
+    def multiply(c, high, low):
+        both = dot(pair_ref[...], high)
+        part = (both[:HALF] + both[HALF:]) + dot(pair_ref[:HALF, :], low)
+        lanes = pl.ds(spot + c * STEP, STEP)
         keep_ref[:, lanes] = part[:QUARTER]
         give_ref[:, lanes] = part[QUARTER:]
+
+    if scaled:
+        for c in range(cols // STEP):
+            lanes = pl.ds(c * STEP, STEP)
+            multiply(c, high_ref[:, lanes], low_ref[:, lanes])
+    else:
+        block = pl.BlockSpec((2 * rows, STEP), lambda i: (0, i))
+
+        def body(high, low):
+            step = pl.program_id(0)
+            for c in range(cols // STEP):
+                @pl.when(step == c)
+                def _():
+                    multiply(c, high[...], low[...])
+
+        pltpu.emit_pipeline(body, grid=(cols // STEP,), in_specs=[block] * 2)(high_ref, low_ref)
 
 
 def product(scaled, me, before, parts, buffer):
@@ -237,9 +257,9 @@
     return call(
         functools.partial(product_kernel, not before, scaled), "product", 4 * rows * width * RANK, 4 * rows * width,
         out_shape=[shaped(QUARTER, width)] * 2 + [shaped(rows, HALF)],
-        in_specs=[SMEM] + [VMEM] * (6 + len(before)), out_specs=[VMEM] * 3,
+        in_specs=[SMEM] + [VMEM] * (4 + len(before)) + [VMEM if scaled else HBM] * 2, out_specs=[VMEM] * 3,
         scratch_shapes=[pltpu.VMEM((HALF, rows), F32)] * 2 + [pltpu.VMEM((RANK, rows), BF16)],
-    )(me, *before, *parts, *buffer)
+    )(me, *before, *parts, *(buffer if scaled else in_hbm(*buffer)))
 
 
 def solved(inverse, wide_ref, out_ref, pair_ref):
@@ -374,31 +394,23 @@
 
         up0, down0 = up0 + got0[0], down0 + got0[1]
         got0 = swap(up0, "col", 2), swap(down0, "col", 1)
-        if not sweep:
-            got1 = swap(up1, "col", 1), swap(down1, "col", 2)
-            up0, down0, got0, up1, down1, got1 = together(up0, down0, got0, up1, down1, got1)
-            up1, down1 = up1 + got1[0], down1 + got1[1]
-            got1 = swap(up1, "col", 2), swap(down1, "col", 1)
-        else:
+        if sweep:
             up1, down1 = left_product(buffer, split1, square1)
-            up0, down0, got0, up1, down1 = together(up0, down0, got0, up1, down1)
-            got1 = swap(up1, "col", 1), swap(down1, "col", 2)
+        up0, down0, got0, up1, down1 = together(up0, down0, got0, up1, down1)
+
         keep0, give0, left0 = product(scaled, me, (), (up0, got0[0], down0, got0[1]), buffer)
-        up1, down1, got1, keep0, give0, left0 = together(up1, down1, got1, keep0, give0, left0)
-
-        core0 = swap(give0, "row", 1)
-        if sweep:
-            up1, down1 = up1 + got1[0], down1 + got1[1]
-            got1 = swap(up1, "col", 2), swap(down1, "col", 1)
-        up1, down1, got1, keep0, core0, left0 = together(up1, down1, got1, keep0, core0, left0)
-
-        part0 = keep0 + core0
+        got1 = swap(up1, "col", 1), swap(down1, "col", 2)
+        keep0, give0, left0, up1, down1, got1 = together(keep0, give0, left0, up1, down1, got1)
+
+        part0 = keep0 + swap(give0, "row", 1)
         pair0 = swap(part0[PART:], "row", 2)
-        keep1, give1, left1 = product(scaled, me, (left0,), (up1, got1[0], down1, got1[1]), buffer)
-        part0, pair0, keep1, give1 = together(part0, pair0, keep1, give1)
+        up1, down1 = up1 + got1[0], down1 + got1[1]
+        got1 = swap(up1, "col", 2), swap(down1, "col", 1)
+        part0, pair0, up1, down1, got1, left0 = together(part0, pair0, up1, down1, got1, left0)
 
         side0 = part0[:PART] + pair0
         cross0 = swap(side0, "row", 4)
+        keep1, give1, left1 = product(scaled, me, (left0,), (up1, got1[0], down1, got1[1]), buffer)
         part1 = keep1 + swap(give1, "row", 1)
         pair1 = swap(part1[PART:], "row", 2)
         side0, cross0, part1, pair1 = together(side0, cross0, part1, pair1)

time: 212 us -> 210 us (level)
  Pallas kernels: 60.7 us -> 70.6 us
  local copies, waits for them, and re-layouts: 8.67 us -> 0.28 us
  waiting for transfers between devices: 95 us -> 91.5 us
    unnamed x21 -> x13, local copies, waits for them, and re-layouts: 8.5 us -> 0.1 us
    pallas_call x4, Pallas kernels: 11.1 us -> 18.4 us  [product(): call(functools.partial(product_kernel, not before, scaled), 'product', 4...]
    ppermute x39, waiting for transfers between devices: 95 us -> 91.5 us  [swap(): return lax.ppermute(x, axis, [(i, i ^ bit) for i in range(size)])]
    pallas_call x1, Pallas kernels: 9.14 us -> 11.7 us  [start(): call(start_kernel, 'start', 6 * rows * cols * RANK, 10 * rows * cols, out...]
  transfers between devices with their start and end apart: 39 -> 39, of which waited for: 29 -> 27; matrix products, arithmetic and copies ran while one was open for 0% -> 0% of each run, Pallas kernels for 19% -> 17%
where the time goes in v2:
time: 210 us; the launch traced here: 209 us
  waiting for transfers between devices  91.5 us (44%)
  Pallas kernels  70.6 us (34%)
  starting transfers between devices  45.4 us (22%)
    ppermute x39, waiting for transfers between devices, swap(): return lax.ppermute(x, axis, [(i, i ^ bit) for i in range(size)])  91.5 us
    ppermute x39, starting transfers between devices, swap(): return lax.ppermute(x, axis, [(i, i ^ bit) for i in range(size)])  45.4 us
    pallas_call x4, Pallas kernels, product(): call(functools.partial(product_kernel, not before, scaled), 'product', 4...  18.4 us
    pallas_call x2, Pallas kernels, second_solve(): call(second_kernel, 'second_solve', 6000000000, 20 * HALF * cols, out_sha...  12.5 us
    pallas_call x1, Pallas kernels, start(): call(start_kernel, 'start', 6 * rows * cols * RANK, 10 * rows * cols, out...  11.7 us
    pallas_call x2, Pallas kernels, first_solve(): call(first_kernel, 'first_solve', 5000000000, 20 * HALF * cols, out_shape...  10.4 us
    pallas_call x2, Pallas kernels, left_product(): call(left_kernel, 'left', 4 * rows * cols * RANK, 4 * rows * cols, out_sh...  6.3 us
    pallas_call x1, Pallas kernels, weight_update(): call(weight_kernel, 'weight', 6 * rows * cols * RANK, 4 * rows * cols, ou...  6.25 us
  transfers between devices with their start and end apart: 39, of which 27 were waited for; matrix products, arithmetic and copies ran while one was open for 0% of the time, Pallas kernels for 17%

profile of v2, /device:TPU:0, one launch (start us, length us, event | category | flops | bytes accessed | tf_op | source)
XLA Modules:
  0.0 209.5 jit_solution(15716435159524056440)
XLA Ops:
  0.6 11.7 %start.1 = (bf16[1024,2048]{1,0:T(8,128)(2,1)}, bf16[1024,2048]{1,0:T(8,128)(2,1)}, f32[512,128]{1,0:T(8,128)S(1)}, f32[512,128]{1,0:T(8,128)S(1)}, f32[512,128]{1,0:T(8,128)S(1)}, /*index=5*/f32[512,128]{1,0:T(8,128)S(1)}) custom-call(f32[1024,2048]{1,0:T(8,128)} %bitcast.6, bf16[1024,2048]{1,0:T(8,128)(2,1)} %bitcast.7, f32[2048,256]{1,0:T(8,128)} %basis_ref.1), custom_call_target="tpu_custom_call" | custom-call | flops 3221225472 | bytes 20971520 | tf_op jit(solution)/shard_map/start/pallas_call | solution.py:171
  12.4 2.9 %collective-permute-start = (f32[512,128]{1,0:T(8,128)S(1)}, f32[512,128]{1,0:T(8,128)S(1)}, u32[]{:S(2)}, u32[]{:S(2)}) collective-permute-start(f32[512,128]{1,0:T(8,128)S(1)} %get-tuple-element.129), channel_id=1, source_target_pairs={{0,1},{1,0},{2,3},{3,2},{4,5},{5,4},{6,7},{7,6},{8,9},{9,8},{10,11... | collective-permute-start | bytes 786440 | tf_op jit(solution)/shard_map/ppermute | solution.py:378
  16.8 4.8 %collective-permute-done = f32[512,128]{1,0:T(8,128)S(1)} collective-permute-done((f32[512,128]{1,0:T(8,128)S(1)}, f32[512,128]{1,0:T(8,128)S(1)}, u32[]{:S(2)}, u32[]{:S(2)}) %collective-permute-start) | collective-permute-done | bytes 262176 | tf_op jit(solution)/shard_map/ppermute | solution.py:378
  25.3 4.7 %collective-permute-done.3.refs_3_ = f32[512,128]{1,0:T(8,128)S(1)} collective-permute-done((f32[512,128]{1,0:T(8,128)S(1)}, f32[512,128]{1,0:T(8,128)S(1)}, u32[]{:S(2)}, u32[]{:S(2)}) %collective-permute-start.3) | collective-permute-done | bytes 262176 | tf_op jit(solution)/shard_map/ppermute | solution.py:378
  33.4 6.0 %product.4 = (f32[64,2176]{1,0:T(8,128)S(1)}, f32[64,2176]{1,0:T(8,128)S(1)}, f32[1024,128]{1,0:T(8,128)S(1)}) custom-call(s32[1]{0:T(128)} %bitcast.me_ref, f32[512,128]{1,0:T(8,128)S(1)} %add.64.refs_0_, f32[512,128]{1,0:T(8,128)S(1)} %collective-permute-done.2.refs_1_, f32[512,128]{1,0:T(8,128)S(1)} %add.65.refs_2_, ...), custom_call_target="tpu_custom_call" | custom-call | flops 2281701376 | bytes 8912896 | tf_op jit(solution)/shard_map/product/pallas_call | solution.py:257
  44.4 6.9 %collective-permute-done.9.refs_4_ = f32[512,128]{1,0:T(8,128)S(1)} collective-permute-done((f32[512,128]{1,0:T(8,128)S(1)}, f32[512,128]{1,0:T(8,128)S(1)}, u32[]{:S(2)}, u32[]{:S(2)}) %collective-permute-start.9) | collective-permute-done | bytes 262176 | tf_op jit(solution)/shard_map/ppermute | solution.py:378
  51.7 7.2 %product.5 = (f32[64,2304]{1,0:T(8,128)S(1)}, f32[64,2304]{1,0:T(8,128)S(1)}, f32[1024,128]{1,0:T(8,128)}) custom-call(s32[1]{0:T(128)} %bitcast.me_ref, f32[1024,128]{1,0:T(8,128)S(1)} %get-tuple-element.153.refs_0_, f32[512,128]{1,0:T(8,128)S(1)} %add.67.refs_1_, f32[512,128]{1,0:T(8,128)S(1)} %collective-permute-done.8.refs_2_, ...), custom_call_target="tpu_custom_call" | custom-call | flops 2415919104 | bytes 9437184 | tf_op jit(solution)/shard_map/product/pallas_call | solution.py:257
  64.2 9.9 %collective-permute-done.10 = f32[32,2176]{1,0:T(8,128)S(1)} collective-permute-done((f32[32,2176]{1,0:T(8,128)S(1)}, f32[32,2176]{1,0:T(8,128)S(1)}, u32[]{:S(2)}, u32[]{:S(2)}) %collective-permute-start.10) | collective-permute-done | bytes 278560 | tf_op jit(solution)/shard_map/ppermute | solution.py:378
  77.7 3.6 %collective-permute-start.13 = (f32[32,2176]{1,0:T(8,128)S(1)}, f32[32,2176]{1,0:T(8,128)S(1)}, u32[]{:S(2)}, u32[]{:S(2)}) collective-permute-start(f32[32,2176]{1,0:T(8,128)S(1)} %add.71), channel_id=1, source_target_pairs={{0,8},{4,12},{8,0},{12,4},{16,24},{20,28},{24,16},{28,20},{1,9},{5... | collective-permute-start | bytes 835592 | tf_op jit(solution)/shard_map/ppermute | solution.py:378
  81.3 8.0 %collective-permute-done.13 = f32[32,2176]{1,0:T(8,128)S(1)} collective-permute-done((f32[32,2176]{1,0:T(8,128)S(1)}, f32[32,2176]{1,0:T(8,128)S(1)}, u32[]{:S(2)}, u32[]{:S(2)}) %collective-permute-start.13) | collective-permute-done | bytes 278560 | tf_op jit(solution)/shard_map/ppermute | solution.py:378
  93.7 5.6 %first_solve.2 = (f32[128,128]{1,0:T(8,128)S(1)}, f32[128,2048]{1,0:T(8,128)S(1)}, f32[128,2048]{1,0:T(8,128)}, bf16[256,2048]{1,0:T(8,128)(2,1)S(1)}, f32[8,128]{1,0:T(8,128)S(1)}) custom-call(s32[1]{0:T(128)} %bitcast.me_ref, f32[64,2176]{1,0:T(8,128)S(1)} %constant_dynamic-update-slice_fusion.mine_ref, f32[64,2176]{1,0:T(8,128)S(1)} %collective-permute-done.16.other_ref), custom_call_target="tpu_custom_call" | custom-call | flops 5000000000 | bytes 5242880 | tf_op jit(solution)/shard_map/first_solve/pallas_call | solution.py:288
  101.4 3.1 %left.2 = (f32[520,128]{1,0:T(8,128)S(1)}, f32[512,128]{1,0:T(8,128)S(1)}) custom-call(bf16[1024,2048]{1,0:T(8,128)(2,1)S(1)} %copy-done, bf16[1024,2048]{1,0:T(8,128)(2,1)S(1)} %copy-done.1, bf16[256,2048]{1,0:T(8,128)(2,1)S(1)} %get-tuple-element.172.factor_ref, f32[8,128]{1,0:T(8,128)S(1)} %get-tuple-element.173.refs_0_), custom_call_target="tpu_custom_call" | custom-call | flops 2147483648 | bytes 8388608 | tf_op jit(solution)/shard_map/left/pallas_call | solution.py:198
  106.6 6.6 %second_solve.2 = (f32[256,256]{1,0:T(8,128)}, f32[128,2048]{1,0:T(8,128)}, bf16[256,2048]{1,0:T(8,128)(2,1)S(1)}, f32[8,128]{1,0:T(8,128)S(1)}) custom-call(s32[1]{0:T(128)} %bitcast.me_ref, f32[64,2304]{1,0:T(8,128)S(1)} %constant_dynamic-update-slice_fusion.2.mine_ref, f32[64,2304]{1,0:T(8,128)S(1)} %collective-permute-done.19.other_ref, ...), custom_call_target="tpu_custom_call" | custom-call | flops 6000000000 | bytes 5242880 | tf_op jit(solution)/shard_map/second_solve/pallas_call | solution.py:312
  116.6 3.2 %left.3 = (f32[520,128]{1,0:T(8,128)S(1)}, f32[512,128]{1,0:T(8,128)S(1)}) custom-call(bf16[1024,2048]{1,0:T(8,128)(2,1)S(1)} %copy-done, bf16[1024,2048]{1,0:T(8,128)(2,1)S(1)} %copy-done.1, bf16[256,2048]{1,0:T(8,128)(2,1)S(1)} %get-tuple-element.186.factor_ref, f32[8,128]{1,0:T(8,128)S(1)} %get-tuple-element.187.refs_0_), custom_call_target="tpu_custom_call" | custom-call | flops 2147483648 | bytes 8388608 | tf_op jit(solution)/shard_map/left/pallas_call | solution.py:198
  126.6 3.4 %collective-permute-done.23 = f32[512,128]{1,0:T(8,128)S(1)} collective-permute-done((f32[512,128]{1,0:T(8,128)S(1)}, f32[512,128]{1,0:T(8,128)S(1)}, u32[]{:S(2)}, u32[]{:S(2)}) %collective-permute-start.23) | collective-permute-done | bytes 262176 | tf_op jit(solution)/shard_map/ppermute | solution.py:378
  134.1 6.9 %collective-permute-done.27.refs_4_ = f32[512,128]{1,0:T(8,128)S(1)} collective-permute-done((f32[512,128]{1,0:T(8,128)S(1)}, f32[512,128]{1,0:T(8,128)S(1)}, u32[]{:S(2)}, u32[]{:S(2)}) %collective-permute-start.27) | collective-permute-done | bytes 262176 | tf_op jit(solution)/shard_map/ppermute | solution.py:378
  141.0 2.8 %product.7 = (f32[64,2304]{1,0:T(8,128)S(1)}, f32[64,2304]{1,0:T(8,128)S(1)}, f32[1024,128]{1,0:T(8,128)S(1)}) custom-call(s32[1]{0:T(128)} %bitcast.me_ref, f32[1024,128]{1,0:T(8,128)S(1)} %get-tuple-element.206.refs_0_.left0_ref, f32[520,128]{1,0:T(8,128)S(1)} %add.77.refs_1_, f32[520,128]{1,0:T(8,128)S(1)} %collective-permute-done.26.refs_2_, ...), custom_call_target="tpu_custom_call" | custom-call | flops 2415919104 | bytes 9437184 | tf_op jit(solution)/shard_map/product/pallas_call | solution.py:257
  150.3 10.1 %collective-permute-done.28 = f32[32,2176]{1,0:T(8,128)S(1)} collective-permute-done((f32[32,2176]{1,0:T(8,128)S(1)}, f32[32,2176]{1,0:T(8,128)S(1)}, u32[]{:S(2)}, u32[]{:S(2)}) %collective-permute-start.28) | collective-permute-done | bytes 278560 | tf_op jit(solution)/shard_map/ppermute | solution.py:378
  164.0 3.6 %collective-permute-start.31 = (f32[32,2176]{1,0:T(8,128)S(1)}, f32[32,2176]{1,0:T(8,128)S(1)}, u32[]{:S(2)}, u32[]{:S(2)}) collective-permute-start(f32[32,2176]{1,0:T(8,128)S(1)} %add.81), channel_id=1, source_target_pairs={{0,8},{4,12},{8,0},{12,4},{16,24},{20,28},{24,16},{28,20},{1,9},{5... | collective-permute-start | bytes 835592 | tf_op jit(solution)/shard_map/ppermute | solution.py:378
  167.6 8.0 %collective-permute-done.31 = f32[32,2176]{1,0:T(8,128)S(1)} collective-permute-done((f32[32,2176]{1,0:T(8,128)S(1)}, f32[32,2176]{1,0:T(8,128)S(1)}, u32[]{:S(2)}, u32[]{:S(2)}) %collective-permute-start.31) | collective-permute-done | bytes 278560 | tf_op jit(solution)/shard_map/ppermute | solution.py:378
  179.1 4.8 %first_solve.3 = (f32[128,128]{1,0:T(8,128)S(1)}, f32[128,2048]{1,0:T(8,128)S(1)}, f32[128,2048]{1,0:T(8,128)S(1)}, bf16[256,2048]{1,0:T(8,128)(2,1)S(1)}, f32[8,128]{1,0:T(8,128)S(1)}) custom-call(s32[1]{0:T(128)} %bitcast.me_ref, f32[64,2176]{1,0:T(8,128)S(1)} %constant_dynamic-update-slice_fusion.4.mine_ref, f32[64,2176]{1,0:T(8,128)S(1)} %collective-permute-done.34.other_ref), custom_call_target="tpu_custom_call" | custom-call | flops 5000000000 | bytes 5242880 | tf_op jit(solution)/shard_map/first_solve/pallas_call | solution.py:288
  188.8 5.9 %second_solve.3 = (f32[256,256]{1,0:T(8,128)S(1)}, f32[128,2048]{1,0:T(8,128)S(1)}, bf16[256,2048]{1,0:T(8,128)(2,1)S(1)}, f32[8,128]{1,0:T(8,128)S(1)}) custom-call(s32[1]{0:T(128)} %bitcast.me_ref, f32[64,2304]{1,0:T(8,128)S(1)} %constant_dynamic-update-slice_fusion.6.mine_ref, f32[64,2304]{1,0:T(8,128)S(1)} %collective-permute-done.35.other_ref, ...), custom_call_target="tpu_custom_call" | custom-call | flops 6000000000 | bytes 5242880 | tf_op jit(solution)/shard_map/second_solve/pallas_call | solution.py:312
  198.2 5.0 %momentum.1 = (f32[1024,2048]{1,0:T(8,128)}, f32[1024,256]{1,0:T(8,128)S(1)}) custom-call(f32[1024,128]{1,0:T(8,128)S(1)} %get-tuple-element.206.refs_0_.left0_ref, f32[1024,128]{1,0:T(8,128)S(1)} %get-tuple-element.211.left1_ref, f32[256,256]{1,0:T(8,128)S(1)} %get-tuple-element.232.inverse_ref, bf16[256,2048]{1,0:T(8,128)(2,1)S(1)} %get-tuple-element.233.pair0_ref, ...), custom_call_target="tpu_custom_call" | custom-call | flops 1073741824 | bytes 8388608 | tf_op jit(solution)/shard_map/momentum/pallas_call | solution.py:338
  203.2 6.2 %weight.1 = (f32[1024,2048]{1,0:T(8,128)}, f32[2048,256]{1,0:T(8,128)}) custom-call(f32[1024,256]{1,0:T(8,128)S(1)} %get-tuple-element.236.ortho_ref, f32[8,256]{1,0:T(8,128)S(1)} %constant_dynamic-update-slice_fusion.8.s0, f32[8,256]{1,0:T(8,128)S(1)} %collective-permute-done.36.s1, f32[8,256]{1,0:T(8,128)S(1)} %collective-permute-done.37.s2, ...), custom_call_target="tpu_custom_call" | custom-call | flops 3221225472 | bytes 8388608 | tf_op jit(solution)/shard_map/weight/pallas_call | solution.py:368
  (110 shorter events, 67.5 us)
Async XLA Ops:
  12.4 9.2 %collective-permute-start = (f32[512,128]{1,0:T(8,128)S(1)}, f32[512,128]{1,0:T(8,128)S(1)}, u32[]{:S(2)}, u32[]{:S(2)}) collective-permute-start(f32[512,128]{1,0:T(8,128)S(1)} %get-tuple-element.129), channel_id=1, source_target_pairs={{0,1},{1,0},{2,3},{3,2},{4,5},{5,4},{6,7},{7,6},{8,9},{9,8},{10,11... | collective-permute-start | bytes 786440 | tf_op jit(solution)/shard_map/ppermute | solution.py:378
  15.3 7.8 %collective-permute-start.1 = (f32[512,128]{1,0:T(8,128)S(1)}, f32[512,128]{1,0:T(8,128)S(1)}, u32[]{:S(2)}, u32[]{:S(2)}) collective-permute-start(f32[512,128]{1,0:T(8,128)S(1)} %get-tuple-element.131), channel_id=1, source_target_pairs={{0,2},{1,3},{2,0},{3,1},{4,6},{5,7},{6,4},{7,5},{8,10},{9,11},{10,... | collective-permute-start | bytes 786440 | tf_op jit(solution)/shard_map/ppermute | solution.py:378
  30.5 8.9 %collective-permute-start.4 = (f32[512,128]{1,0:T(8,128)S(1)}, f32[512,128]{1,0:T(8,128)S(1)}, u32[]{:S(2)}, u32[]{:S(2)}) collective-permute-start(f32[512,128]{1,0:T(8,128)S(1)} %get-tuple-element.146), channel_id=1, source_target_pairs={{0,1},{1,0},{2,3},{3,2},{4,5},{5,4},{6,7},{7,6},{8,9},{9,8},{10,11... | collective-permute-start | bytes 786440 | tf_op jit(solution)/shard_map/ppermute | solution.py:378
  41.5 10.2 %collective-permute-start.7 = (f32[32,2176]{1,0:T(8,128)S(1)}, f32[32,2176]{1,0:T(8,128)S(1)}, u32[]{:S(2)}, u32[]{:S(2)}) collective-permute-start(f32[32,2176]{1,0:T(8,128)S(1)} %slice.32), channel_id=1, source_target_pairs={{0,8},{4,12},{8,0},{12,4},{16,24},{20,28},{24,16},{28,20},{1,9},{5... | collective-permute-start | bytes 835592 | tf_op jit(solution)/shard_map/ppermute | solution.py:378
  43.2 8.1 %collective-permute-start.9 = (f32[512,128]{1,0:T(8,128)S(1)}, f32[512,128]{1,0:T(8,128)S(1)}, u32[]{:S(2)}, u32[]{:S(2)}) collective-permute-start(f32[512,128]{1,0:T(8,128)S(1)} %add.68.refs_3_), channel_id=1, source_target_pairs={{0,1},{1,0},{2,3},{3,2},{4,5},{5,4},{6,7},{7,6},{8,9},{9,8},{10,11... | collective-permute-start | bytes 786440 | tf_op jit(solution)/shard_map/ppermute | solution.py:378
  43.9 7.9 %collective-permute-start.8 = (f32[512,128]{1,0:T(8,128)S(1)}, f32[512,128]{1,0:T(8,128)S(1)}, u32[]{:S(2)}, u32[]{:S(2)}) collective-permute-start(f32[512,128]{1,0:T(8,128)S(1)} %add.67.refs_1_), channel_id=1, source_target_pairs={{0,2},{1,3},{2,0},{3,1},{4,6},{5,7},{6,4},{7,5},{8,10},{9,11},{10,... | collective-permute-start | bytes 786440 | tf_op jit(solution)/shard_map/ppermute | solution.py:378
  61.0 15.1 %collective-permute-start.12 = (f32[32,2304]{1,0:T(8,128)S(1)}, f32[32,2304]{1,0:T(8,128)S(1)}, u32[]{:S(2)}, u32[]{:S(2)}) collective-permute-start(f32[32,2304]{1,0:T(8,128)S(1)} %slice.33), channel_id=1, source_target_pairs={{0,8},{4,12},{8,0},{12,4},{16,24},{20,28},{24,16},{28,20},{1,9},{5... | collective-permute-start | bytes 884744 | tf_op jit(solution)/shard_map/ppermute | solution.py:378
  61.5 12.5 %collective-permute-start.10 = (f32[32,2176]{1,0:T(8,128)S(1)}, f32[32,2176]{1,0:T(8,128)S(1)}, u32[]{:S(2)}, u32[]{:S(2)}) collective-permute-start(f32[32,2176]{1,0:T(8,128)S(1)} %slice_add_fusion.3), channel_id=1, source_target_pairs={{0,16},{4,20},{8,24},{12,28},{16,0},{20,4},{24,8},{28,12},{1,17},{... | collective-permute-start | bytes 835592 | tf_op jit(solution)/shard_map/ppermute | solution.py:378
  76.1 15.5 %collective-permute-start.14 = (f32[32,2304]{1,0:T(8,128)S(1)}, f32[32,2304]{1,0:T(8,128)S(1)}, u32[]{:S(2)}, u32[]{:S(2)}) collective-permute-start(f32[32,2304]{1,0:T(8,128)S(1)} %slice_add_fusion.1), channel_id=1, source_target_pairs={{0,16},{4,20},{8,24},{12,28},{16,0},{20,4},{24,8},{28,12},{1,17},{... | collective-permute-start | bytes 884744 | tf_op jit(solution)/shard_map/ppermute | solution.py:378
  77.7 11.7 %collective-permute-start.13 = (f32[32,2176]{1,0:T(8,128)S(1)}, f32[32,2176]{1,0:T(8,128)S(1)}, u32[]{:S(2)}, u32[]{:S(2)}) collective-permute-start(f32[32,2176]{1,0:T(8,128)S(1)} %add.71), channel_id=1, source_target_pairs={{0,8},{4,12},{8,0},{12,4},{16,24},{20,28},{24,16},{28,20},{1,9},{5... | collective-permute-start | bytes 835592 | tf_op jit(solution)/shard_map/ppermute | solution.py:378
  91.8 9.5 %collective-permute-start.15 = (f32[32,2304]{1,0:T(8,128)S(1)}, f32[32,2304]{1,0:T(8,128)S(1)}, u32[]{:S(2)}, u32[]{:S(2)}) collective-permute-start(f32[32,2304]{1,0:T(8,128)S(1)} %add.73), channel_id=1, source_target_pairs={{0,8},{4,12},{8,0},{12,4},{16,24},{20,28},{24,16},{28,20},{1,9},{5... | collective-permute-start | bytes 884744 | tf_op jit(solution)/shard_map/ppermute | solution.py:378
  104.6 8.6 %collective-permute-start.18 = (f32[512,128]{1,0:T(8,128)S(1)}, f32[512,128]{1,0:T(8,128)S(1)}, u32[]{:S(2)}, u32[]{:S(2)}) collective-permute-start(f32[512,128]{1,0:T(8,128)S(1)} %get-tuple-element.184), channel_id=1, source_target_pairs={{0,2},{1,3},{2,0},{3,1},{4,6},{5,7},{6,4},{7,5},{8,10},{9,11},{10,... | collective-permute-start | bytes 786440 | tf_op jit(solution)/shard_map/ppermute | solution.py:378
  105.1 8.3 %collective-permute-start.17 = (f32[520,128]{1,0:T(8,128)S(1)}, f32[520,128]{1,0:T(8,128)S(1)}, u32[]{:S(2)}, u32[]{:S(2)}) collective-permute-start(f32[520,128]{1,0:T(8,128)S(1)} %get-tuple-element.182), channel_id=1, source_target_pairs={{0,1},{1,0},{2,3},{3,2},{4,5},{5,4},{6,7},{7,6},{8,9},{9,8},{10,11... | collective-permute-start | bytes 798728 | tf_op jit(solution)/shard_map/ppermute | solution.py:378
  113.5 9.0 %collective-permute-start.20 = (f32[520,128]{1,0:T(8,128)S(1)}, f32[520,128]{1,0:T(8,128)S(1)}, u32[]{:S(2)}, u32[]{:S(2)}) collective-permute-start(f32[520,128]{1,0:T(8,128)S(1)} %add.74.refs_0_), channel_id=1, source_target_pairs={{0,2},{1,3},{2,0},{3,1},{4,6},{5,7},{6,4},{7,5},{8,10},{9,11},{10,... | collective-permute-start | bytes 798728 | tf_op jit(solution)/shard_map/ppermute | solution.py:378
  122.6 7.5 %collective-permute-start.22 = (f32[520,128]{1,0:T(8,128)S(1)}, f32[520,128]{1,0:T(8,128)S(1)}, u32[]{:S(2)}, u32[]{:S(2)}) collective-permute-start(f32[520,128]{1,0:T(8,128)S(1)} %get-tuple-element.201), channel_id=1, source_target_pairs={{0,1},{1,0},{2,3},{3,2},{4,5},{5,4},{6,7},{7,6},{8,9},{9,8},{10,11... | collective-permute-start | bytes 798728 | tf_op jit(solution)/shard_map/ppermute | solution.py:378
  132.1 8.9 %collective-permute-start.25 = (f32[32,2176]{1,0:T(8,128)S(1)}, f32[32,2176]{1,0:T(8,128)S(1)}, u32[]{:S(2)}, u32[]{:S(2)}) collective-permute-start(f32[32,2176]{1,0:T(8,128)S(1)} %slice.34), channel_id=1, source_target_pairs={{0,8},{4,12},{8,0},{12,4},{16,24},{20,28},{24,16},{28,20},{1,9},{5... | collective-permute-start | bytes 835592 | tf_op jit(solution)/shard_map/ppermute | solution.py:378
  132.5 8.5 %collective-permute-start.26 = (f32[520,128]{1,0:T(8,128)S(1)}, f32[520,128]{1,0:T(8,128)S(1)}, u32[]{:S(2)}, u32[]{:S(2)}) collective-permute-start(f32[520,128]{1,0:T(8,128)S(1)} %add.77.refs_1_), channel_id=1, source_target_pairs={{0,2},{1,3},{2,0},{3,1},{4,6},{5,7},{6,4},{7,5},{8,10},{9,11},{10,... | collective-permute-start | bytes 798728 | tf_op jit(solution)/shard_map/ppermute | solution.py:378
  133.2 7.9 %collective-permute-start.27 = (f32[512,128]{1,0:T(8,128)S(1)}, f32[512,128]{1,0:T(8,128)S(1)}, u32[]{:S(2)}, u32[]{:S(2)}) collective-permute-start(f32[512,128]{1,0:T(8,128)S(1)} %add.78.refs_3_), channel_id=1, source_target_pairs={{0,1},{1,0},{2,3},{3,2},{4,5},{5,4},{6,7},{7,6},{8,9},{9,8},{10,11... | collective-permute-start | bytes 786440 | tf_op jit(solution)/shard_map/ppermute | solution.py:378
  146.0 15.1 %collective-permute-start.30 = (f32[32,2304]{1,0:T(8,128)S(1)}, f32[32,2304]{1,0:T(8,128)S(1)}, u32[]{:S(2)}, u32[]{:S(2)}) collective-permute-start(f32[32,2304]{1,0:T(8,128)S(1)} %slice.35), channel_id=1, source_target_pairs={{0,8},{4,12},{8,0},{12,4},{16,24},{20,28},{24,16},{28,20},{1,9},{5... | collective-permute-start | bytes 884744 | tf_op jit(solution)/shard_map/ppermute | solution.py:378
  147.8 12.5 %collective-permute-start.28 = (f32[32,2176]{1,0:T(8,128)S(1)}, f32[32,2176]{1,0:T(8,128)S(1)}, u32[]{:S(2)}, u32[]{:S(2)}) collective-permute-start(f32[32,2176]{1,0:T(8,128)S(1)} %slice_add_fusion.2), channel_id=1, source_target_pairs={{0,16},{4,20},{8,24},{12,28},{16,0},{20,4},{24,8},{28,12},{1,17},{... | collective-permute-start | bytes 835592 | tf_op jit(solution)/shard_map/ppermute | solution.py:378
  161.1 15.9 %collective-permute-start.32 = (f32[32,2304]{1,0:T(8,128)S(1)}, f32[32,2304]{1,0:T(8,128)S(1)}, u32[]{:S(2)}, u32[]{:S(2)}) collective-permute-start(f32[32,2304]{1,0:T(8,128)S(1)} %slice_add_fusion), channel_id=1, source_target_pairs={{0,16},{4,20},{8,24},{12,28},{16,0},{20,4},{24,8},{28,12},{1,17},{... | collective-permute-start | bytes 884744 | tf_op jit(solution)/shard_map/ppermute | solution.py:378
  164.0 11.7 %collective-permute-start.31 = (f32[32,2176]{1,0:T(8,128)S(1)}, f32[32,2176]{1,0:T(8,128)S(1)}, u32[]{:S(2)}, u32[]{:S(2)}) collective-permute-start(f32[32,2176]{1,0:T(8,128)S(1)} %add.81), channel_id=1, source_target_pairs={{0,8},{4,12},{8,0},{12,4},{16,24},{20,28},{24,16},{28,20},{1,9},{5... | collective-permute-start | bytes 835592 | tf_op jit(solution)/shard_map/ppermute | solution.py:378
  177.2 9.5 %collective-permute-start.33 = (f32[32,2304]{1,0:T(8,128)S(1)}, f32[32,2304]{1,0:T(8,128)S(1)}, u32[]{:S(2)}, u32[]{:S(2)}) collective-permute-start(f32[32,2304]{1,0:T(8,128)S(1)} %add.83), channel_id=1, source_target_pairs={{0,8},{4,12},{8,0},{12,4},{16,24},{20,28},{24,16},{28,20},{1,9},{5... | collective-permute-start | bytes 884744 | tf_op jit(solution)/shard_map/ppermute | solution.py:378
  194.7 8.5 %collective-permute-start.38 = (f32[8,256]{1,0:T(8,128)S(1)}, f32[8,256]{1,0:T(8,128)S(1)}, u32[]{:S(2)}, u32[]{:S(2)}) collective-permute-start(f32[8,256]{1,0:T(8,128)S(1)} %constant_dynamic-update-slice_fusion.8.s0), channel_id=1, source_target_pairs={{0,3},{1,2},{2,1},{3,0},{4,7},{5,6},{6,5},{7,4},{8,11},{9,10},{10,... | collective-permute-start | bytes 24584 | tf_op jit(solution)/shard_map/ppermute | solution.py:378
  (19 other events, 127.2 us)

commit v3 on v1

--- a/solution.py
+++ b/solution.py
@@ -56,6 +56,7 @@
 
 
 VMEM = pl.BlockSpec(memory_space=pltpu.VMEM)
+HBM = pl.BlockSpec(memory_space=pltpu.HBM)
 SMEM = pl.BlockSpec(memory_space=pltpu.SMEM)
 
 
@@ -128,7 +129,7 @@
         out_ref[pl.ds(pl.multiple_of((me ^ b) * PART, PART), PART), :] = block
 
 
-def start_kernel(momentum_ref, gradient_ref, basis_ref, high_ref, low_ref, up0, down0, up1, down1, pair_ref):
+def start_kernel(me_ref, momentum_ref, gradient_ref, basis_ref, high_ref, low_ref, up0, down0, up1, down1, pair_ref):
     rows, cols = momentum_ref.shape
     count = up0.shape[0] // TILE
 
@@ -162,15 +163,14 @@
     )(momentum_ref, gradient_ref, basis_ref)
 
 
-def start(*args):
+def start(me, *args):
     rows, cols = args[0].shape
-    high, low, *parts = call(
+    return call(
         start_kernel, "start", 6 * rows * cols * RANK, 6 * rows * cols,
-        out_shape=[shaped(rows, cols, dtype=BF16)] * 2 + [shaped(rows // 2, HALF)] * 4,
-        in_specs=[pl.BlockSpec(memory_space=pltpu.HBM)] * 3, out_specs=[VMEM] * 6,
+        out_shape=[pltpu.VMEM((rows, cols), BF16)] * 2 + [shaped(rows // 2, HALF)] * 4,
+        in_specs=[SMEM] + [HBM] * 3, out_specs=[VMEM] * 6,
         scratch_shapes=[pltpu.VMEM((cols, 2 * RANK), BF16)],
-    )(*(pltpu.with_memory_space_constraint(x, pltpu.HBM) for x in args))
-    return (*(pltpu.with_memory_space_constraint(x, pltpu.VMEM) for x in (high, low)), *parts)
+    )(me, *(pltpu.with_memory_space_constraint(x, pltpu.HBM) for x in args))
 
 
 def left_kernel(high_ref, low_ref, factor_ref, *refs):
@@ -365,7 +365,7 @@
 def tuned(momentum, gradient, weight, right_basis):
     row = lax.axis_index("row")
     me = (2 * (row & 1) + ((row >> 1) & 1)).astype(jnp.int32)[None]
-    high, low, up0, down0, up1, down1 = start(momentum[0], gradient[0], right_basis)
+    high, low, up0, down0, up1, down1 = start(me, momentum[0], gradient[0], right_basis)
     buffer = (high, low)
     got0 = swap(up0, "col", 1), swap(down0, "col", 2)
     up0, down0, got0, up1, down1 = together(up0, down0, got0, up1, down1)
@@ -374,32 +374,27 @@
 
         up0, down0 = up0 + got0[0], down0 + got0[1]
         got0 = swap(up0, "col", 2), swap(down0, "col", 1)
-        if not sweep:
-            got1 = swap(up1, "col", 1), swap(down1, "col", 2)
-            up0, down0, got0, up1, down1, got1 = together(up0, down0, got0, up1, down1, got1)
-            up1, down1 = up1 + got1[0], down1 + got1[1]
-            got1 = swap(up1, "col", 2), swap(down1, "col", 1)
-        else:
+        if sweep:
             up1, down1 = left_product(buffer, split1, square1)
-            up0, down0, got0, up1, down1 = together(up0, down0, got0, up1, down1)
-            got1 = swap(up1, "col", 1), swap(down1, "col", 2)
+        up0, down0, got0, up1, down1 = together(up0, down0, got0, up1, down1)
+
         keep0, give0, left0 = product(scaled, me, (), (up0, got0[0], down0, got0[1]), buffer)
-        up1, down1, got1, keep0, give0, left0 = together(up1, down1, got1, keep0, give0, left0)
-
-        core0 = swap(give0, "row", 1)
-        if sweep:
-            up1, down1 = up1 + got1[0], down1 + got1[1]
-            got1 = swap(up1, "col", 2), swap(down1, "col", 1)
-        up1, down1, got1, keep0, core0, left0 = together(up1, down1, got1, keep0, core0, left0)
-
-        part0 = keep0 + core0
+        got1 = swap(up1, "col", 1), swap(down1, "col", 2)
+        keep0, give0, left0, up1, down1, got1 = together(keep0, give0, left0, up1, down1, got1)
+
+        part0 = keep0 + swap(give0, "row", 1)
         pair0 = swap(part0[PART:], "row", 2)
+        up1, down1 = up1 + got1[0], down1 + got1[1]
+        got1 = swap(up1, "col", 2), swap(down1, "col", 1)
         keep1, give1, left1 = product(scaled, me, (left0,), (up1, got1[0], down1, got1[1]), buffer)
         part0, pair0, keep1, give1 = together(part0, pair0, keep1, give1)
 
+        core1 = swap(give1, "row", 1)
+        part0, pair0, keep1, core1 = together(part0, pair0, keep1, core1)
+
         side0 = part0[:PART] + pair0
         cross0 = swap(side0, "row", 4)
-        part1 = keep1 + swap(give1, "row", 1)
+        part1 = keep1 + core1
         pair1 = swap(part1[PART:], "row", 2)
         side0, cross0, part1, pair1 = together(side0, cross0, part1, pair1)
 

time: 212 us -> 198 us (0.934)
  waiting for transfers between devices: 95 us -> 86.3 us
  local copies, waits for them, and re-layouts: 8.67 us -> 0.27 us
  starting transfers between devices: 45.4 us -> 48.8 us
    ppermute x39, waiting for transfers between devices: 95 us -> 86.3 us  [swap(): return lax.ppermute(x, axis, [(i, i ^ bit) for i in range(size)])]
    unnamed x21 -> x9, local copies, waits for them, and re-layouts: 8.5 us -> 0.09 us
    ppermute x39, starting transfers between devices: 45.4 us -> 48.8 us  [swap(): return lax.ppermute(x, axis, [(i, i ^ bit) for i in range(size)])]
  transfers between devices with their start and end apart: 39 -> 39, of which waited for: 29 -> 27; matrix products, arithmetic and copies ran while one was open for 0% -> 0% of each run, Pallas kernels for 19% -> 20%
where the time goes in v3:
time: 198 us
  waiting for transfers between devices  86.3 us (44%)
  Pallas kernels  60.7 us (31%)
  starting transfers between devices  48.8 us (25%)
    ppermute x39, waiting for transfers between devices, swap(): return lax.ppermute(x, axis, [(i, i ^ bit) for i in range(size)])  86.3 us
    ppermute x39, starting transfers between devices, swap(): return lax.ppermute(x, axis, [(i, i ^ bit) for i in range(size)])  48.8 us
    pallas_call x2, Pallas kernels, second_solve(): call(second_kernel, 'second_solve', 6000000000, 20 * HALF * cols, out_sha...  12.5 us
    pallas_call x4, Pallas kernels, product(): call(functools.partial(product_kernel, not before, scaled), 'product', 4...  11.2 us
    pallas_call x2, Pallas kernels, first_solve(): call(first_kernel, 'first_solve', 5000000000, 20 * HALF * cols, out_shape...  10.4 us
    pallas_call x1, Pallas kernels, start(): call(start_kernel, 'start', 6 * rows * cols * RANK, 6 * rows * cols, out_...  9.15 us
    pallas_call x2, Pallas kernels, left_product(): call(left_kernel, 'left', 4 * rows * cols * RANK, 4 * rows * cols, out_sh...  6.32 us
    pallas_call x1, Pallas kernels, weight_update(): call(weight_kernel, 'weight', 6 * rows * cols * RANK, 4 * rows * cols, ou...  6.25 us
  transfers between devices with their start and end apart: 39, of which 27 were waited for; matrix products, arithmetic and copies ran while one was open for 0% of the time, Pallas kernels for 20%

profile of v3, /device:TPU:0, one launch (start us, length us, event | category | flops | bytes accessed | tf_op | source)
XLA Modules:
  0.0 197.9 jit_solution(14529103879599088866)
XLA Ops:
  0.6 9.1 %start.1 = (bf16[1024,2048]{1,0:T(8,128)(2,1)S(1)}, bf16[1024,2048]{1,0:T(8,128)(2,1)S(1)}, f32[512,128]{1,0:T(8,128)S(1)}, f32[512,128]{1,0:T(8,128)S(1)}, f32[...) custom-call(s32[1]{0:T(128)} %bitcast.me_ref, f32[1024,2048]{1,0:T(8,128)} %bitcast.6, bf16[1024,2048]{1,0:T(8,128)(2,1)} %bitcast.7, ...), custom_call_target="tpu_custom_call" | custom-call | flops 3221225472 | bytes 12582912 | tf_op jit(solution)/shard_map/start/pallas_call | solution.py:168
  9.8 3.0 %collective-permute-start = (f32[512,128]{1,0:T(8,128)S(1)}, f32[512,128]{1,0:T(8,128)S(1)}, u32[]{:S(2)}, u32[]{:S(2)}) collective-permute-start(f32[512,128]{1,0:T(8,128)S(1)} %get-tuple-element.131), channel_id=1, source_target_pairs={{0,1},{1,0},{2,3},{3,2},{4,5},{5,4},{6,7},{7,6},{8,9},{9,8},{10,11... | collective-permute-start | bytes 786440 | tf_op jit(solution)/shard_map/ppermute | solution.py:358
  14.3 4.8 %collective-permute-done = f32[512,128]{1,0:T(8,128)S(1)} collective-permute-done((f32[512,128]{1,0:T(8,128)S(1)}, f32[512,128]{1,0:T(8,128)S(1)}, u32[]{:S(2)}, u32[]{:S(2)}) %collective-permute-start) | collective-permute-done | bytes 262176 | tf_op jit(solution)/shard_map/ppermute | solution.py:358
  22.8 4.7 %collective-permute-done.3.refs_3_ = f32[512,128]{1,0:T(8,128)S(1)} collective-permute-done((f32[512,128]{1,0:T(8,128)S(1)}, f32[512,128]{1,0:T(8,128)S(1)}, u32[]{:S(2)}, u32[]{:S(2)}) %collective-permute-start.3) | collective-permute-done | bytes 262176 | tf_op jit(solution)/shard_map/ppermute | solution.py:358
  39.8 4.8 %collective-permute-done.9.refs_4_ = f32[512,128]{1,0:T(8,128)S(1)} collective-permute-done((f32[512,128]{1,0:T(8,128)S(1)}, f32[512,128]{1,0:T(8,128)S(1)}, u32[]{:S(2)}, u32[]{:S(2)}) %collective-permute-start.9) | collective-permute-done | bytes 262176 | tf_op jit(solution)/shard_map/ppermute | solution.py:358
  45.0 3.5 %product.5 = (f32[64,2304]{1,0:T(8,128)S(1)}, f32[64,2304]{1,0:T(8,128)S(1)}, f32[1024,128]{1,0:T(8,128)}) custom-call(s32[1]{0:T(128)} %bitcast.me_ref, f32[1024,128]{1,0:T(8,128)S(1)} %get-tuple-element.148.refs_0_, f32[512,128]{1,0:T(8,128)S(1)} %add.67.refs_1_, f32[512,128]{1,0:T(8,128)S(1)} %collective-permute-done.8.refs_2_, ...), custom_call_target="tpu_custom_call" | custom-call | flops 2415919104 | bytes 9437184 | tf_op jit(solution)/shard_map/product/pallas_call | solution.py:237
  52.2 2.7 %collective-permute-start.11 = (f32[32,2176]{1,0:T(8,128)S(1)}, f32[32,2176]{1,0:T(8,128)S(1)}, u32[]{:S(2)}, u32[]{:S(2)}) collective-permute-start(f32[32,2176]{1,0:T(8,128)S(1)} %slice_add_fusion.3), channel_id=1, source_target_pairs={{0,16},{4,20},{8,24},{12,28},{16,0},{20,4},{24,8},{28,12},{1,17},{... | collective-permute-start | bytes 835592 | tf_op jit(solution)/shard_map/ppermute | solution.py:358
  54.9 9.9 %collective-permute-done.11 = f32[32,2176]{1,0:T(8,128)S(1)} collective-permute-done((f32[32,2176]{1,0:T(8,128)S(1)}, f32[32,2176]{1,0:T(8,128)S(1)}, u32[]{:S(2)}, u32[]{:S(2)}) %collective-permute-start.11) | collective-permute-done | bytes 278560 | tf_op jit(solution)/shard_map/ppermute | solution.py:358
  65.7 2.6 %collective-permute-start.14 = (f32[32,2304]{1,0:T(8,128)S(1)}, f32[32,2304]{1,0:T(8,128)S(1)}, u32[]{:S(2)}, u32[]{:S(2)}) collective-permute-start(f32[32,2304]{1,0:T(8,128)S(1)} %slice_add_fusion.1), channel_id=1, source_target_pairs={{0,16},{4,20},{8,24},{12,28},{16,0},{20,4},{24,8},{28,12},{1,17},{... | collective-permute-start | bytes 884744 | tf_op jit(solution)/shard_map/ppermute | solution.py:358
  70.8 9.1 %collective-permute-done.13 = f32[32,2176]{1,0:T(8,128)S(1)} collective-permute-done((f32[32,2176]{1,0:T(8,128)S(1)}, f32[32,2176]{1,0:T(8,128)S(1)}, u32[]{:S(2)}, u32[]{:S(2)}) %collective-permute-start.13) | collective-permute-done | bytes 278560 | tf_op jit(solution)/shard_map/ppermute | solution.py:358
  83.3 5.6 %first_solve.2 = (f32[128,128]{1,0:T(8,128)S(1)}, f32[128,2048]{1,0:T(8,128)S(1)}, f32[128,2048]{1,0:T(8,128)}, bf16[256,2048]{1,0:T(8,128)(2,1)S(1)}, f32[8,128]{1,0:T(8,128)S(1)}) custom-call(s32[1]{0:T(128)} %bitcast.me_ref, f32[64,2176]{1,0:T(8,128)S(1)} %constant_dynamic-update-slice_fusion.mine_ref, f32[64,2176]{1,0:T(8,128)S(1)} %collective-permute-done.16.other_ref), custom_call_target="tpu_custom_call" | custom-call | flops 5000000000 | bytes 5242880 | tf_op jit(solution)/shard_map/first_solve/pallas_call | solution.py:268
  91.0 3.1 %left.2 = (f32[520,128]{1,0:T(8,128)S(1)}, f32[512,128]{1,0:T(8,128)S(1)}) custom-call(bf16[1024,2048]{1,0:T(8,128)(2,1)S(1)} %get-tuple-element.125.refs_4_.refs_5_.high_ref, bf16[1024,2048]{1,0:T(8,128)(2,1)S(1)} %get-tuple-element.126.refs_5_.refs_6_.low_ref, bf16[256,2048]{1,0:T(8,128)(2,1)S(1)} %get-tuple-element.175.factor_ref, ...), custom_call_target="tpu_custom_call" | custom-call | flops 2147483648 | bytes 8388608 | tf_op jit(solution)/shard_map/left/pallas_call | solution.py:194
  97.1 6.6 %second_solve.2 = (f32[256,256]{1,0:T(8,128)}, f32[128,2048]{1,0:T(8,128)}, bf16[256,2048]{1,0:T(8,128)(2,1)S(1)}, f32[8,128]{1,0:T(8,128)S(1)}) custom-call(s32[1]{0:T(128)} %bitcast.me_ref, f32[64,2304]{1,0:T(8,128)S(1)} %constant_dynamic-update-slice_fusion.2.mine_ref, f32[64,2304]{1,0:T(8,128)S(1)} %collective-permute-done.19.other_ref, ...), custom_call_target="tpu_custom_call" | custom-call | flops 6000000000 | bytes 5242880 | tf_op jit(solution)/shard_map/second_solve/pallas_call | solution.py:292
  106.1 3.2 %left.3 = (f32[520,128]{1,0:T(8,128)S(1)}, f32[512,128]{1,0:T(8,128)S(1)}) custom-call(bf16[1024,2048]{1,0:T(8,128)(2,1)S(1)} %get-tuple-element.125.refs_4_.refs_5_.high_ref, bf16[1024,2048]{1,0:T(8,128)(2,1)S(1)} %get-tuple-element.126.refs_5_.refs_6_.low_ref, bf16[256,2048]{1,0:T(8,128)(2,1)S(1)} %get-tuple-element.189.factor_ref, ...), custom_call_target="tpu_custom_call" | custom-call | flops 2147483648 | bytes 8388608 | tf_op jit(solution)/shard_map/left/pallas_call | solution.py:194
  109.3 2.8 %collective-permute-done.21.refs_3_ = f32[512,128]{1,0:T(8,128)S(1)} collective-permute-done((f32[512,128]{1,0:T(8,128)S(1)}, f32[512,128]{1,0:T(8,128)S(1)}, u32[]{:S(2)}, u32[]{:S(2)}) %collective-permute-start.21) | collective-permute-done | bytes 262176 | tf_op jit(solution)/shard_map/ppermute | solution.py:358
  123.7 6.1 %collective-permute-done.25.refs_4_ = f32[512,128]{1,0:T(8,128)S(1)} collective-permute-done((f32[512,128]{1,0:T(8,128)S(1)}, f32[512,128]{1,0:T(8,128)S(1)}, u32[]{:S(2)}, u32[]{:S(2)}) %collective-permute-start.25) | collective-permute-done | bytes 262176 | tf_op jit(solution)/shard_map/ppermute | solution.py:358
  129.8 2.9 %product.7 = (f32[64,2304]{1,0:T(8,128)S(1)}, f32[64,2304]{1,0:T(8,128)S(1)}, f32[1024,128]{1,0:T(8,128)S(1)}) custom-call(s32[1]{0:T(128)} %bitcast.me_ref, f32[1024,128]{1,0:T(8,128)S(1)} %get-tuple-element.202.refs_0_.left0_ref, f32[520,128]{1,0:T(8,128)S(1)} %add.76.refs_1_, f32[520,128]{1,0:T(8,128)S(1)} %collective-permute-done.24.refs_2_, ...), custom_call_target="tpu_custom_call" | custom-call | flops 2415919104 | bytes 9437184 | tf_op jit(solution)/shard_map/product/pallas_call | solution.py:237
  138.2 10.6 %collective-permute-done.29 = f32[32,2176]{1,0:T(8,128)S(1)} collective-permute-done((f32[32,2176]{1,0:T(8,128)S(1)}, f32[32,2176]{1,0:T(8,128)S(1)}, u32[]{:S(2)}, u32[]{:S(2)}) %collective-permute-start.29) | collective-permute-done | bytes 278560 | tf_op jit(solution)/shard_map/ppermute | solution.py:358
  154.8 9.2 %collective-permute-done.31 = f32[32,2176]{1,0:T(8,128)S(1)} collective-permute-done((f32[32,2176]{1,0:T(8,128)S(1)}, f32[32,2176]{1,0:T(8,128)S(1)}, u32[]{:S(2)}, u32[]{:S(2)}) %collective-permute-start.31) | collective-permute-done | bytes 278560 | tf_op jit(solution)/shard_map/ppermute | solution.py:358
  167.5 4.8 %first_solve.3 = (f32[128,128]{1,0:T(8,128)S(1)}, f32[128,2048]{1,0:T(8,128)S(1)}, f32[128,2048]{1,0:T(8,128)S(1)}, bf16[256,2048]{1,0:T(8,128)(2,1)S(1)}, f32[8,128]{1,0:T(8,128)S(1)}) custom-call(s32[1]{0:T(128)} %bitcast.me_ref, f32[64,2176]{1,0:T(8,128)S(1)} %constant_dynamic-update-slice_fusion.4.mine_ref, f32[64,2176]{1,0:T(8,128)S(1)} %collective-permute-done.34.other_ref), custom_call_target="tpu_custom_call" | custom-call | flops 5000000000 | bytes 5242880 | tf_op jit(solution)/shard_map/first_solve/pallas_call | solution.py:268
  172.3 2.8 %collective-permute-done.33 = f32[32,2304]{1,0:T(8,128)S(1)} collective-permute-done((f32[32,2304]{1,0:T(8,128)S(1)}, f32[32,2304]{1,0:T(8,128)S(1)}, u32[]{:S(2)}, u32[]{:S(2)}) %collective-permute-start.33) | collective-permute-done | bytes 294944 | tf_op jit(solution)/shard_map/ppermute | solution.py:358
  177.2 5.9 %second_solve.3 = (f32[256,256]{1,0:T(8,128)S(1)}, f32[128,2048]{1,0:T(8,128)S(1)}, bf16[256,2048]{1,0:T(8,128)(2,1)S(1)}, f32[8,128]{1,0:T(8,128)S(1)}) custom-call(s32[1]{0:T(128)} %bitcast.me_ref, f32[64,2304]{1,0:T(8,128)S(1)} %constant_dynamic-update-slice_fusion.6.mine_ref, f32[64,2304]{1,0:T(8,128)S(1)} %collective-permute-done.35.other_ref, ...), custom_call_target="tpu_custom_call" | custom-call | flops 6000000000 | bytes 5242880 | tf_op jit(solution)/shard_map/second_solve/pallas_call | solution.py:292
  186.6 5.0 %momentum.1 = (f32[1024,2048]{1,0:T(8,128)}, f32[1024,256]{1,0:T(8,128)S(1)}) custom-call(f32[1024,128]{1,0:T(8,128)S(1)} %get-tuple-element.202.refs_0_.left0_ref, f32[1024,128]{1,0:T(8,128)S(1)} %get-tuple-element.207.left1_ref, f32[256,256]{1,0:T(8,128)S(1)} %get-tuple-element.236.inverse_ref, bf16[256,2048]{1,0:T(8,128)(2,1)S(1)} %get-tuple-element.237.pair0_ref, ...), custom_call_target="tpu_custom_call" | custom-call | flops 1073741824 | bytes 8388608 | tf_op jit(solution)/shard_map/momentum/pallas_call | solution.py:318
  191.6 6.2 %weight.1 = (f32[1024,2048]{1,0:T(8,128)}, f32[2048,256]{1,0:T(8,128)}) custom-call(f32[1024,256]{1,0:T(8,128)S(1)} %get-tuple-element.240.ortho_ref, f32[8,256]{1,0:T(8,128)S(1)} %constant_dynamic-update-slice_fusion.8.s0, f32[8,256]{1,0:T(8,128)S(1)} %collective-permute-done.36.s1, f32[8,256]{1,0:T(8,128)S(1)} %collective-permute-done.37.s2, ...), custom_call_target="tpu_custom_call" | custom-call | flops 3221225472 | bytes 8388608 | tf_op jit(solution)/shard_map/weight/pallas_call | solution.py:348
  (106 shorter events, 68.0 us)
Async XLA Ops:
  9.8 9.3 %collective-permute-start = (f32[512,128]{1,0:T(8,128)S(1)}, f32[512,128]{1,0:T(8,128)S(1)}, u32[]{:S(2)}, u32[]{:S(2)}) collective-permute-start(f32[512,128]{1,0:T(8,128)S(1)} %get-tuple-element.131), channel_id=1, source_target_pairs={{0,1},{1,0},{2,3},{3,2},{4,5},{5,4},{6,7},{7,6},{8,9},{9,8},{10,11... | collective-permute-start | bytes 786440 | tf_op jit(solution)/shard_map/ppermute | solution.py:358
  12.8 7.8 %collective-permute-start.1 = (f32[512,128]{1,0:T(8,128)S(1)}, f32[512,128]{1,0:T(8,128)S(1)}, u32[]{:S(2)}, u32[]{:S(2)}) collective-permute-start(f32[512,128]{1,0:T(8,128)S(1)} %get-tuple-element.133), channel_id=1, source_target_pairs={{0,2},{1,3},{2,0},{3,1},{4,6},{5,7},{6,4},{7,5},{8,10},{9,11},{10,... | collective-permute-start | bytes 786440 | tf_op jit(solution)/shard_map/ppermute | solution.py:358
  35.8 8.8 %collective-permute-start.9 = (f32[512,128]{1,0:T(8,128)S(1)}, f32[512,128]{1,0:T(8,128)S(1)}, u32[]{:S(2)}, u32[]{:S(2)}) collective-permute-start(f32[512,128]{1,0:T(8,128)S(1)} %add.68.refs_3_), channel_id=1, source_target_pairs={{0,1},{1,0},{2,3},{3,2},{4,5},{5,4},{6,7},{7,6},{8,9},{9,8},{10,11... | collective-permute-start | bytes 786440 | tf_op jit(solution)/shard_map/ppermute | solution.py:358
  36.5 8.5 %collective-permute-start.8 = (f32[512,128]{1,0:T(8,128)S(1)}, f32[512,128]{1,0:T(8,128)S(1)}, u32[]{:S(2)}, u32[]{:S(2)}) collective-permute-start(f32[512,128]{1,0:T(8,128)S(1)} %add.67.refs_1_), channel_id=1, source_target_pairs={{0,2},{1,3},{2,0},{3,1},{4,6},{5,7},{6,4},{7,5},{8,10},{9,11},{10,... | collective-permute-start | bytes 786440 | tf_op jit(solution)/shard_map/ppermute | solution.py:358
  38.1 10.4 %collective-permute-start.7 = (f32[32,2176]{1,0:T(8,128)S(1)}, f32[32,2176]{1,0:T(8,128)S(1)}, u32[]{:S(2)}, u32[]{:S(2)}) collective-permute-start(f32[32,2176]{1,0:T(8,128)S(1)} %slice.32), channel_id=1, source_target_pairs={{0,8},{4,12},{8,0},{12,4},{16,24},{20,28},{24,16},{28,20},{1,9},{5... | collective-permute-start | bytes 835592 | tf_op jit(solution)/shard_map/ppermute | solution.py:358
  50.6 15.1 %collective-permute-start.12 = (f32[32,2304]{1,0:T(8,128)S(1)}, f32[32,2304]{1,0:T(8,128)S(1)}, u32[]{:S(2)}, u32[]{:S(2)}) collective-permute-start(f32[32,2304]{1,0:T(8,128)S(1)} %slice.33), channel_id=1, source_target_pairs={{0,8},{4,12},{8,0},{12,4},{16,24},{20,28},{24,16},{28,20},{1,9},{5... | collective-permute-start | bytes 884744 | tf_op jit(solution)/shard_map/ppermute | solution.py:358
  52.2 12.5 %collective-permute-start.11 = (f32[32,2176]{1,0:T(8,128)S(1)}, f32[32,2176]{1,0:T(8,128)S(1)}, u32[]{:S(2)}, u32[]{:S(2)}) collective-permute-start(f32[32,2176]{1,0:T(8,128)S(1)} %slice_add_fusion.3), channel_id=1, source_target_pairs={{0,16},{4,20},{8,24},{12,28},{16,0},{20,4},{24,8},{28,12},{1,17},{... | collective-permute-start | bytes 835592 | tf_op jit(solution)/shard_map/ppermute | solution.py:358
  65.7 15.5 %collective-permute-start.14 = (f32[32,2304]{1,0:T(8,128)S(1)}, f32[32,2304]{1,0:T(8,128)S(1)}, u32[]{:S(2)}, u32[]{:S(2)}) collective-permute-start(f32[32,2304]{1,0:T(8,128)S(1)} %slice_add_fusion.1), channel_id=1, source_target_pairs={{0,16},{4,20},{8,24},{12,28},{16,0},{20,4},{24,8},{28,12},{1,17},{... | collective-permute-start | bytes 884744 | tf_op jit(solution)/shard_map/ppermute | solution.py:358
  68.3 11.7 %collective-permute-start.13 = (f32[32,2176]{1,0:T(8,128)S(1)}, f32[32,2176]{1,0:T(8,128)S(1)}, u32[]{:S(2)}, u32[]{:S(2)}) collective-permute-start(f32[32,2176]{1,0:T(8,128)S(1)} %add.71), channel_id=1, source_target_pairs={{0,8},{4,12},{8,0},{12,4},{16,24},{20,28},{24,16},{28,20},{1,9},{5... | collective-permute-start | bytes 835592 | tf_op jit(solution)/shard_map/ppermute | solution.py:358
  81.4 9.5 %collective-permute-start.15 = (f32[32,2304]{1,0:T(8,128)S(1)}, f32[32,2304]{1,0:T(8,128)S(1)}, u32[]{:S(2)}, u32[]{:S(2)}) collective-permute-start(f32[32,2304]{1,0:T(8,128)S(1)} %add.73), channel_id=1, source_target_pairs={{0,8},{4,12},{8,0},{12,4},{16,24},{20,28},{24,16},{28,20},{1,9},{5... | collective-permute-start | bytes 884744 | tf_op jit(solution)/shard_map/ppermute | solution.py:358
  94.1 9.5 %collective-permute-start.18 = (f32[512,128]{1,0:T(8,128)S(1)}, f32[512,128]{1,0:T(8,128)S(1)}, u32[]{:S(2)}, u32[]{:S(2)}) collective-permute-start(f32[512,128]{1,0:T(8,128)S(1)} %get-tuple-element.187), channel_id=1, source_target_pairs={{0,2},{1,3},{2,0},{3,1},{4,6},{5,7},{6,4},{7,5},{8,10},{9,11},{10,... | collective-permute-start | bytes 786440 | tf_op jit(solution)/shard_map/ppermute | solution.py:358
  95.7 8.3 %collective-permute-start.17 = (f32[520,128]{1,0:T(8,128)S(1)}, f32[520,128]{1,0:T(8,128)S(1)}, u32[]{:S(2)}, u32[]{:S(2)}) collective-permute-start(f32[520,128]{1,0:T(8,128)S(1)} %get-tuple-element.185), channel_id=1, source_target_pairs={{0,1},{1,0},{2,3},{3,2},{4,5},{5,4},{6,7},{7,6},{8,9},{9,8},{10,11... | collective-permute-start | bytes 798728 | tf_op jit(solution)/shard_map/ppermute | solution.py:358
  104.0 8.0 %collective-permute-start.20 = (f32[520,128]{1,0:T(8,128)S(1)}, f32[520,128]{1,0:T(8,128)S(1)}, u32[]{:S(2)}, u32[]{:S(2)}) collective-permute-start(f32[520,128]{1,0:T(8,128)S(1)} %add.74.refs_0_), channel_id=1, source_target_pairs={{0,2},{1,3},{2,0},{3,1},{4,6},{5,7},{6,4},{7,5},{8,10},{9,11},{10,... | collective-permute-start | bytes 798728 | tf_op jit(solution)/shard_map/ppermute | solution.py:358
  112.1 7.6 %collective-permute-start.22 = (f32[520,128]{1,0:T(8,128)S(1)}, f32[520,128]{1,0:T(8,128)S(1)}, u32[]{:S(2)}, u32[]{:S(2)}) collective-permute-start(f32[520,128]{1,0:T(8,128)S(1)} %get-tuple-element.203), channel_id=1, source_target_pairs={{0,1},{1,0},{2,3},{3,2},{4,5},{5,4},{6,7},{7,6},{8,9},{9,8},{10,11... | collective-permute-start | bytes 798728 | tf_op jit(solution)/shard_map/ppermute | solution.py:358
  119.7 10.1 %collective-permute-start.24 = (f32[520,128]{1,0:T(8,128)S(1)}, f32[520,128]{1,0:T(8,128)S(1)}, u32[]{:S(2)}, u32[]{:S(2)}) collective-permute-start(f32[520,128]{1,0:T(8,128)S(1)} %add.76.refs_1_), channel_id=1, source_target_pairs={{0,2},{1,3},{2,0},{3,1},{4,6},{5,7},{6,4},{7,5},{8,10},{9,11},{10,... | collective-permute-start | bytes 798728 | tf_op jit(solution)/shard_map/ppermute | solution.py:358
  121.3 8.5 %collective-permute-start.25 = (f32[512,128]{1,0:T(8,128)S(1)}, f32[512,128]{1,0:T(8,128)S(1)}, u32[]{:S(2)}, u32[]{:S(2)}) collective-permute-start(f32[512,128]{1,0:T(8,128)S(1)} %add.77.refs_3_), channel_id=1, source_target_pairs={{0,1},{1,0},{2,3},{3,2},{4,5},{5,4},{6,7},{7,6},{8,9},{9,8},{10,11... | collective-permute-start | bytes 786440 | tf_op jit(solution)/shard_map/ppermute | solution.py:358
  122.3 10.4 %collective-permute-start.27 = (f32[32,2176]{1,0:T(8,128)S(1)}, f32[32,2176]{1,0:T(8,128)S(1)}, u32[]{:S(2)}, u32[]{:S(2)}) collective-permute-start(f32[32,2176]{1,0:T(8,128)S(1)} %slice.34), channel_id=1, source_target_pairs={{0,8},{4,12},{8,0},{12,4},{16,24},{20,28},{24,16},{28,20},{1,9},{5... | collective-permute-start | bytes 835592 | tf_op jit(solution)/shard_map/ppermute | solution.py:358
  134.8 15.1 %collective-permute-start.30 = (f32[32,2304]{1,0:T(8,128)S(1)}, f32[32,2304]{1,0:T(8,128)S(1)}, u32[]{:S(2)}, u32[]{:S(2)}) collective-permute-start(f32[32,2304]{1,0:T(8,128)S(1)} %slice.35), channel_id=1, source_target_pairs={{0,8},{4,12},{8,0},{12,4},{16,24},{20,28},{24,16},{28,20},{1,9},{5... | collective-permute-start | bytes 884744 | tf_op jit(solution)/shard_map/ppermute | solution.py:358
  136.3 12.5 %collective-permute-start.29 = (f32[32,2176]{1,0:T(8,128)S(1)}, f32[32,2176]{1,0:T(8,128)S(1)}, u32[]{:S(2)}, u32[]{:S(2)}) collective-permute-start(f32[32,2176]{1,0:T(8,128)S(1)} %slice_add_fusion.2), channel_id=1, source_target_pairs={{0,16},{4,20},{8,24},{12,28},{16,0},{20,4},{24,8},{28,12},{1,17},{... | collective-permute-start | bytes 835592 | tf_op jit(solution)/shard_map/ppermute | solution.py:358
  149.9 15.5 %collective-permute-start.32 = (f32[32,2304]{1,0:T(8,128)S(1)}, f32[32,2304]{1,0:T(8,128)S(1)}, u32[]{:S(2)}, u32[]{:S(2)}) collective-permute-start(f32[32,2304]{1,0:T(8,128)S(1)} %slice_add_fusion), channel_id=1, source_target_pairs={{0,16},{4,20},{8,24},{12,28},{16,0},{20,4},{24,8},{28,12},{1,17},{... | collective-permute-start | bytes 884744 | tf_op jit(solution)/shard_map/ppermute | solution.py:358
  152.4 11.7 %collective-permute-start.31 = (f32[32,2176]{1,0:T(8,128)S(1)}, f32[32,2176]{1,0:T(8,128)S(1)}, u32[]{:S(2)}, u32[]{:S(2)}) collective-permute-start(f32[32,2176]{1,0:T(8,128)S(1)} %add.81), channel_id=1, source_target_pairs={{0,8},{4,12},{8,0},{12,4},{16,24},{20,28},{24,16},{28,20},{1,9},{5... | collective-permute-start | bytes 835592 | tf_op jit(solution)/shard_map/ppermute | solution.py:358
  165.6 9.5 %collective-permute-start.33 = (f32[32,2304]{1,0:T(8,128)S(1)}, f32[32,2304]{1,0:T(8,128)S(1)}, u32[]{:S(2)}, u32[]{:S(2)}) collective-permute-start(f32[32,2304]{1,0:T(8,128)S(1)} %add.83), channel_id=1, source_target_pairs={{0,8},{4,12},{8,0},{12,4},{16,24},{20,28},{24,16},{28,20},{1,9},{5... | collective-permute-start | bytes 884744 | tf_op jit(solution)/shard_map/ppermute | solution.py:358
  183.1 8.5 %collective-permute-start.38 = (f32[8,256]{1,0:T(8,128)S(1)}, f32[8,256]{1,0:T(8,128)S(1)}, u32[]{:S(2)}, u32[]{:S(2)}) collective-permute-start(f32[8,256]{1,0:T(8,128)S(1)} %constant_dynamic-update-slice_fusion.8.s0), channel_id=1, source_target_pairs={{0,3},{1,2},{2,1},{3,0},{4,7},{5,6},{6,5},{7,4},{8,11},{9,10},{10,... | collective-permute-start | bytes 24584 | tf_op jit(solution)/shard_map/ppermute | solution.py:358
  184.0 7.6 %collective-permute-start.37 = (f32[8,256]{1,0:T(8,128)S(1)}, f32[8,256]{1,0:T(8,128)S(1)}, u32[]{:S(2)}, u32[]{:S(2)}) collective-permute-start(f32[8,256]{1,0:T(8,128)S(1)} %constant_dynamic-update-slice_fusion.8.s0), channel_id=1, source_target_pairs={{0,2},{1,3},{2,0},{3,1},{4,6},{5,7},{6,4},{7,5},{8,10},{9,11},{10,... | collective-permute-start | bytes 24584 | tf_op jit(solution)/shard_map/ppermute | solution.py:358
  (17 other events, 108.2 us)
